TPU v7x, 32 devices: a whole 2x2x4 slice. The times are simulated.
32 devices in a mesh: rep: 4 (over z), fsdp: 4 (over y, x), seq: 2 (over core).
Axes of the slice: x: 2, y: 2, z: 4, core: 2. Of those that a mesh axis runs over, the one named last changes fastest.
Arguments:
- tokens: bfloat16 [2, 16, 1024, 768], P(None, ('rep', 'fsdp'), 'seq'), may hold values from -6 to 6
- cotangent: bfloat16 [2, 16, 1024, 768], P(None, ('rep', 'fsdp'), 'seq'), may hold values from -6 to 6
- segments: int32 [2, 16, 1024], P(None, ('rep', 'fsdp')), may hold values from 0 to 3, as said below
- input_weight: float32 [768, 3328], P(('fsdp', 'seq')), may hold values from -0.21875 to 0.21875
- output_weight: float32 [1536, 768], P(('fsdp', 'seq')), may hold values from -0.15625 to 0.15625
- small_values: float32 [29768], replicated, may hold values from -12 to 2, as said below
- input_momentum: float32 [768, 3328], P(('fsdp', 'seq')), may hold values from -160 to 160
- output_momentum: float32 [1536, 768], P(('fsdp', 'seq')), may hold values from -160 to 160
- small_momentum: float32 [29768], replicated, may hold values from -16 to 16
- input_error: float32 [4, 768, 3328], P('rep', ('fsdp', 'seq')), may hold values from -1357.645 to 1357.645
- output_error: float32 [4, 1536, 768], P('rep', ('fsdp', 'seq')), may hold values from -1357.645 to 1357.645
- input_start: float32 [3328, 8], replicated, may hold values from -6 to 6
- output_start: float32 [768, 8], replicated, may hold values from -6 to 6
Outputs:
- output: bfloat16 [2, 16, 1024, 768], P(None, ('rep', 'fsdp'), 'seq')
- input_grad: bfloat16 [2, 16, 1024, 768], P(None, ('rep', 'fsdp'), 'seq')
- new_input_weight: float32 [768, 3328], P(('fsdp', 'seq'))
- new_output_weight: float32 [1536, 768], P(('fsdp', 'seq'))
- new_input_momentum: float32 [768, 3328], P(('fsdp', 'seq'))
- new_output_momentum: float32 [1536, 768], P(('fsdp', 'seq'))
- new_small_values: float32 [29768], replicated
- new_small_momentum: float32 [29768], replicated
- input_left: float32 [768, 8], P(('fsdp', 'seq'))
- input_right: float32 [3328, 8], replicated
- output_left: float32 [1536, 8], P(('fsdp', 'seq'))
- output_right: float32 [768, 8], replicated
- new_input_error: float32 [4, 768, 3328], P('rep', ('fsdp', 'seq'))
- new_output_error: float32 [4, 1536, 768], P('rep', ('fsdp', 'seq'))
Inputs may be any that keep to these rules, and one draw needn't show every extreme that they name: `segments`: within each sequence the ids never fall and run from 0 to 3: every sequence holds exactly 4 documents of 1 to 512 tokens, one of them exactly 512 tokens. `small_values`: the small parameters lie within this range.
All inputs are finite; a program needn't handle non-finite values.
Results may differ from a plain program's by a relative error of at most 0.012.
Values may be sent and summed in bfloat16 or wider, within the bound.
A program may use at most 192 MiB of HBM per device.

v0:
```python
from functools import partial
import math

import jax
import jax.numpy as jnp
from jax import lax
from jax.experimental import pallas as pl
from jax.experimental.pallas import tpu as pltpu
from jax.sharding import PartitionSpec as P

D = 768
INNER = 1536
HEADS = 24
HEADDIM = 64
STATE = 128
CONV = 4
PROJ = 3328
XBC = 1792

EPS = 1e-05
MOMENTUM = 0.9
HIGH = lax.Precision.HIGHEST
F32 = jnp.float32
BF16 = jnp.bfloat16
HP = 32
CH = 128
HALO = 16
TILE = 256
SUB = 16
ROWS = 256
SPAN = 128 + HALO
NEG = -1e30
VMEM_LIMIT = 63 * 2**20
MESH = pl.DeviceIdType.MESH

BEFORE = 3
LEAD = 128
BIAS, RATE, SKIP = 0, 1, 2
AT_CONV = D + D * HEADS
AT_GATE = AT_CONV + (CONV + 1) * XBC
AT_HEADS = AT_GATE + INNER


def nn(a, b):
    return lax.dot_general(a, b, (((1,), (0,)), ((), ())), preferred_element_type=F32)


def nt(a, b):
    return lax.dot_general(a, b, (((1,), (1,)), ((), ())), preferred_element_type=F32)


def tn(a, b):
    return lax.dot_general(a, b, (((0,), (0,)), ((), ())), preferred_element_type=F32)


def nn_high(a, b):
    return lax.dot_general(
        a, b, (((1,), (0,)), ((), ())), precision=HIGH, preferred_element_type=F32
    )


def nt_high(a, b):
    return lax.dot_general(
        a, b, (((1,), (1,)), ((), ())), precision=HIGH, preferred_element_type=F32
    )


def tn_high(a, b):
    return lax.dot_general(
        a, b, (((0,), (0,)), ((), ())), precision=HIGH, preferred_element_type=F32
    )


def softplus(v):
    return jnp.maximum(v, 0.0) + jnp.log1p(jnp.exp(-jnp.abs(v)))


def sigmoid(v):
    return 0.5 + 0.5 * jnp.tanh(0.5 * v)


def triangle(extent):
    return jnp.where(
        lax.broadcasted_iota(jnp.int32, (extent, extent), 0)
        <= lax.broadcasted_iota(jnp.int32, (extent, extent), 1),
        1.0,
        0.0,
    )


def column(heads_ref, row):
    return heads_ref[...].T[:HP, row : row + 1]


def square_of(row):
    return jnp.broadcast_to(row, (128, 128)).T


def params(semantics, **more):
    return pltpu.CompilerParams(
        dimension_semantics=semantics, vmem_limit_bytes=VMEM_LIMIT, **more
    )


def piece(*shape):
    return pl.BlockSpec((1,) + shape, lambda i: (i,) + (0,) * len(shape))


def whole(shape, ranks=1):
    index = (lambda i: (0,) * len(shape)) if ranks == 1 else (lambda i, k: (0,) * len(shape))
    return pl.BlockSpec(shape, index, pipeline_mode=pl.Buffered(1))


def unpack_small(rows_ref, gain_ref, conv_ref, gate_ref, heads_ref):
    for q in range(D // 128):
        gain_ref[:, q * 128 : q * 128 + 128] = rows_ref[q : q + 1, :]
    at = AT_CONV // 128
    for k in range(CONV + 1):
        for q in range(XBC // 128):
            conv_ref[k : k + 1, q * 128 : q * 128 + 128] = rows_ref[at : at + 1, :]
            at += 1
    gate_ref[...] = rows_ref[at : at + INNER // 128, :]
    row = jnp.broadcast_to(rows_ref[at + INNER // 128 : at + INNER // 128 + 1, :], (8, 128))
    place = lax.broadcasted_iota(jnp.int32, (8, 128), 0)
    heads = jnp.zeros((8, 128), F32)
    for k in range(3):
        moved = row if k == 0 else pltpu.roll(row, 128 - k * HEADS, 1)
        heads = jnp.where(place == k, moved, heads)
    lane = lax.broadcasted_iota(jnp.int32, (8, 128), 1)
    heads_ref[...] = jnp.where(lane < HEADS, heads, 0.0)


def unpack_documents(seg_ref, docs_ref, later):
    n, _, extent = docs_ref.shape
    length = extent - LEAD
    place = lax.broadcasted_iota(jnp.int32, (8, extent), 0)
    for i in range(n):
        ids = jnp.broadcast_to(seg_ref[i].astype(F32), (8, seg_ref.shape[2]))
        ahead, behind = jnp.full((8, LEAD), -1.0, F32), jnp.full((8, LEAD), -3.0, F32)
        ids = jnp.concatenate([ahead, ids, behind], axis=1)
        total = ids.shape[1]
        docs = jnp.zeros((8, extent), F32)
        for row, offset in enumerate((0, 1, 2, 3, -1, -2, -3)):
            moved = ids if offset == 0 else pltpu.roll(ids, (-offset) % total, 1)
            here = jnp.where(later, moved[:, length : length + extent], moved[:, :extent])
            docs = jnp.where(place == row, here, docs)
        docs_ref[i] = docs


def gather_kernel(
    nf, w_ref, tok_ref, small_ref, seg_ref,
    o_ref, halo_ref, gain_ref, conv_ref, gate_ref, heads_ref, docs_ref,
    mine, near, local, send, recv,
):
    r, f, s = lax.axis_index("rep"), lax.axis_index("fsdp"), lax.axis_index("seq")
    other = (r, f, 1 - s)
    if nf == 4:
        fx, fy = f + 1 - 2 * lax.rem(f, 2), lax.rem(f + 2, 4)
        fd = lax.rem(fx + 2, 4)
        far = [(r, fx, s), (r, fy, s)]
    else:
        far = [(r, lax.rem(f + j, nf), s) for j in range(1, nf)]
    barrier = pltpu.get_barrier_semaphore()
    for device in far + [other]:
        pl.semaphore_signal(barrier, inc=1, device_id=device, device_id_type=MESH)
    mine[...] = w_ref[:, INNER:].astype(BF16)
    near[...] = tok_ref[:, tok_ref.shape[1] - HALO :, :]
    pl.semaphore_wait(barrier, len(far) + 1)
    copies = []

    def start(src, dst, device):
        k = len(copies)
        copy = pltpu.make_async_remote_copy(
            src, dst, send.at[k], recv.at[k], device_id=device, device_id_type=MESH
        )
        copy.start()
        copies.append(copy)
        return copy

    def block(owner):
        return o_ref.at[owner * 2 + s]

    own = pltpu.make_async_copy(mine, block(f), local)
    own.start()
    if nf == 4:
        x_dev, y_dev = far
        half = mine.shape[0] // 2
        low, high = pl.ds(0, half), pl.ds(half, half)
        from_x, from_y, from_d = block(fx), block(fy), block(fd)
        x_low = start(mine.at[low], block(f).at[low], x_dev)
        y_high = start(mine.at[high], block(f).at[high], y_dev)
        x_high = start(mine.at[high], block(f).at[high], x_dev)
        y_low = start(mine.at[low], block(f).at[low], y_dev)
        late = [start(mine, block(f), other), start(near, halo_ref, other)]
        unpack_small(small_ref, gain_ref, conv_ref, gate_ref, heads_ref)
        unpack_documents(seg_ref, docs_ref, s == 1)
        x_low.wait_recv()
        d_low = start(from_x.at[low], from_x.at[low], y_dev)
        y_high.wait_recv()
        d_high = start(from_y.at[high], from_y.at[high], x_dev)
        x_high.wait_recv()
        late.append(start(from_x, from_x, other))
        y_low.wait_recv()
        late.append(start(from_y, from_y, other))
        d_low.wait_recv()
        late.append(start(from_d.at[low], from_d.at[low], other))
        d_high.wait_recv()
        late.append(start(from_d.at[high], from_d.at[high], other))
    else:
        first = [start(mine, block(f), device) for device in far]
        late = [start(mine, block(f), other), start(near, halo_ref, other)]
        unpack_small(small_ref, gain_ref, conv_ref, gate_ref, heads_ref)
        unpack_documents(seg_ref, docs_ref, s == 1)
        for j, copy in enumerate(first):
            copy.wait_recv()
            source = block(lax.rem(f - 1 - j + nf, nf))
            late.append(start(source, source, other))
    for copy in late:
        copy.wait_recv()
    for copy in copies:
        copy.wait_send()
    own.wait()


def gather_raw(weight, tokens, small_rows, segments):
    nf = lax.axis_size("fsdp")
    rows = weight.shape[0]
    n, length, _ = tokens.shape
    vmem = pl.BlockSpec(memory_space=pltpu.VMEM)
    dma = pltpu.SemaphoreType.DMA
    count = 12 if nf == 4 else 2 * nf
    full, *rest = pl.pallas_call(
        partial(gather_kernel, nf),
        out_shape=[
            jax.ShapeDtypeStruct((2 * nf, rows, XBC), BF16),
            jax.ShapeDtypeStruct((n, HALO, D), BF16),
            jax.ShapeDtypeStruct((1, D), F32),
            jax.ShapeDtypeStruct((CONV + 1, XBC), F32),
            jax.ShapeDtypeStruct((INNER // 128, 128), F32),
            jax.ShapeDtypeStruct((8, 128), F32),
            jax.ShapeDtypeStruct((n, 8, LEAD + length), F32),
        ],
        in_specs=[vmem] * 4,
        out_specs=[pl.BlockSpec(memory_space=pl.ANY)] + [vmem] * 6,
        scratch_shapes=[
            pltpu.VMEM((rows, XBC), BF16),
            pltpu.VMEM((n, HALO, D), BF16),
            dma,
            dma((count,)),
            dma((count,)),
        ],
        compiler_params=pltpu.CompilerParams(
            collective_id=1, has_side_effects=True, vmem_limit_bytes=VMEM_LIMIT
        ),
        name="gather_raw",
    )(weight, tokens, small_rows, segments)
    return full.reshape(2 * nf * rows, XBC), *rest


def enter_kernel(
    tok_ref, halo_ref, gain_ref, wraw_ref, dlow_ref, conv_ref, heads_ref, docs_ref,
    normed_ref, turned_ref, raw_ref, dsilu_ref, val_ref, wr_ref, draw_ref, delta_ref, send_ref,
    ext, moved, act, shift,
):
    length = tok_ref.shape[1]
    gain = gain_ref[...]
    for start, rows, src in ((0, HALO, halo_ref), (HALO, length, tok_ref)):
        for b in range(0, rows, 128):
            n = min(128, rows - b)
            x = src[0, b : b + n, :].astype(F32)
            scale = lax.rsqrt(jnp.mean(x * x, axis=-1, keepdims=True) + EPS)
            ext[start + b : start + b + n, :] = (x * scale * gain).astype(BF16)
    normed = ext[HALO:, :]
    normed_ref[0] = normed
    turned_ref[0] = normed.T
    own = docs_ref[0, 0:1, LEAD:]
    rows = lax.broadcasted_iota(jnp.int32, (128, SPAN), 0)
    cols = lax.broadcasted_iota(jnp.int32, (128, SPAN), 1)
    for j in range(1, CONV):
        same = jnp.where(docs_ref[0, BEFORE + j : BEFORE + j + 1, LEAD:] == own, 1.0, 0.0)
        for b in range(0, length, 128):
            here = square_of(same[:, b : b + 128])
            here = jnp.concatenate([here, here[:, : SPAN - 128]], axis=1)
            shift[b // 128, (j - 1) * 128 : j * 128, :] = jnp.where(
                cols == rows + (HALO - j), here, 0.0
            ).astype(BF16)

    draw = nt(dlow_ref[...], normed) + column(heads_ref, BIAS)
    delta = softplus(draw)
    draw_ref[0] = draw
    delta_ref[0] = delta
    totals = nn_high(-jnp.exp(column(heads_ref, RATE)) * delta, triangle(length))
    keep = jnp.where(own == own[:, length - 1 :], 1.0, 0.0)
    weight = jnp.exp(totals[:, length - 1 :] - totals) * keep * delta
    tiles = XBC // TILE
    blocks = length // 128

    def span_of(c):
        return slice(c * TILE, (c + 1) * TILE)

    def project(c):
        if c < tiles:
            raw_ref[0, :, span_of(c)] = nn(ext[...], wraw_ref[:, span_of(c)]).astype(BF16)

    def move(c):
        if c < tiles:
            for i in range(blocks):
                moved[c % 2 * blocks + i] = nn(
                    shift[i], raw_ref[0, i * 128 : i * 128 + SPAN, span_of(c)]
                )

    project(0)
    project(1)
    move(0)
    for c in range(tiles):
        span = span_of(c)
        project(c + 2)
        move(c + 1)
        for b in range(0, length, 128):
            slot = c % 2 * blocks + b // 128
            for half in range(0, TILE, 128):
                hc = slice(c * TILE + half, c * TILE + half + 128)
                lanes = slice(half, half + 128)
                w = conv_ref[:, hc]
                for q in range(0, 128, 64):
                    z = w[4:5] + w[3:4] * raw_ref[0, HALO + b + q : HALO + b + q + 64, hc].astype(F32)
                    for j in range(1, CONV):
                        at = (j - 1) * 128 + q
                        z = z + w[3 - j : 4 - j] * moved[slot, at : at + 64, lanes]
                    sig = sigmoid(z)
                    silu = z * sig
                    act[c % 2, b + q : b + q + 64, lanes] = silu
                    dsilu_ref[0, b + q : b + q + 64, hc] = (sig + silu * (1.0 - sig)).astype(BF16)
        if c < INNER // TILE:
            val_ref[0, span, :] = act[c % 2].T.astype(BF16)
        else:
            wr_ref[0] = act[c % 2].astype(BF16)

    writers = wr_ref[0, :, :STATE]
    for h in range(HEADS):
        rows = slice(h * HEADDIM, (h + 1) * HEADDIM)
        scaled = val_ref[0, rows, :].astype(F32) * weight[h : h + 1, :]
        send_ref[0, rows, :] = nn(scaled.astype(BF16), writers).astype(BF16)


def enter(tokens, halo, gain, wraw, dlow, conv, heads, docs):
    n, length, _ = tokens.shape
    outs = [
        ((n, length, D), BF16),
        ((n, D, length), BF16),
        ((n, length + HALO, XBC), BF16),
        ((n, length, XBC), BF16),
        ((n, INNER, length), BF16),
        ((n, length, 2 * STATE), BF16),
        ((n, HP, length), F32),
        ((n, HP, length), F32),
        ((n, INNER, STATE), BF16),
    ]
    return pl.pallas_call(
        enter_kernel,
        grid=(n,),
        in_specs=[
            piece(length, D), piece(HALO, D), whole(gain.shape), whole(wraw.shape),
            whole(dlow.shape), whole(conv.shape), whole(heads.shape), piece(*docs.shape[1:]),
        ],
        out_specs=[piece(*s[1:]) for s, _ in outs],
        out_shape=[jax.ShapeDtypeStruct(s, t) for s, t in outs],
        scratch_shapes=[
            pltpu.VMEM((length + HALO, D), BF16),
            pltpu.VMEM((2 * (length // 128), (CONV - 1) * 128, TILE), F32),
            pltpu.VMEM((2, length, TILE), F32),
            pltpu.VMEM((length // 128, (CONV - 1) * 128, SPAN), BF16),
        ],
        compiler_params=params(("arbitrary",)),
        name="enter",
    )(tokens, halo, gain, wraw, dlow, conv, heads, docs)


def chunk_terms(delta, rate, docs):
    own = docs[0:1, :]
    before = docs[BEFORE + 1 : BEFORE + 2, 0:1]
    last = docs[0:1, CH - 1 :]
    decay = -jnp.exp(rate) * delta
    totals = nn_high(decay, triangle(CH))
    end = totals[:, CH - 1 :]
    fade = jnp.exp(totals) * jnp.where(own == before, 1.0, 0.0)
    to_end = jnp.exp(end - totals) * jnp.where(own == last, 1.0, 0.0)
    passing = jnp.exp(end) * jnp.where(last == before, 1.0, 0.0)
    together = square_of(own) == own
    first = lax.broadcasted_iota(jnp.int32, (CH, CH), 0)
    second = lax.broadcasted_iota(jnp.int32, (CH, CH), 1)
    barred = jnp.where(together & (first <= second), 0.0, NEG)
    reach = jnp.where(together & (first >= second), 1.0, 0.0)
    return decay, totals, fade, to_end, passing, barred, reach


def forward_kernel(
    val_ref, w_ref, r_ref, delta_ref, heads_ref, docs_ref, in_ref,
    y_ref, start_ref,
    state, off, fresh,
):
    state[...] = in_ref[0].astype(F32)
    rate = column(heads_ref, RATE)
    for k in range(val_ref.shape[2] // CH):
        lanes = slice(k * CH, (k + 1) * CH)
        writers, readers = w_ref[0, lanes, :], r_ref[0, lanes, :]
        delta = delta_ref[0, :, lanes]
        _, totals, fade, to_end, passing, barred, _ = chunk_terms(
            delta, rate, docs_ref[0, :, LEAD + k * CH : LEAD + (k + 1) * CH]
        )
        columns = totals.T
        scores = nt(writers, readers)
        low_state = state[...].astype(BF16)
        start_ref[0, k] = low_state
        off[...] = nt(low_state, readers)
        for h in range(HEADS):
            rows = slice(h * HEADDIM, (h + 1) * HEADDIM)
            mixing = jnp.exp(totals[h : h + 1, :] - columns[:, h : h + 1] + barred) * scores
            scaled = val_ref[0, rows, lanes].astype(F32) * delta[h : h + 1, :]
            fresh[rows, :] = (scaled * to_end[h : h + 1, :]).astype(BF16)
            inside = nn(scaled.astype(BF16), mixing.astype(BF16))
            y_ref[0, rows, lanes] = inside + off[rows, :] * fade[h : h + 1, :]
        gained = nn(fresh[...], writers)
        for h in range(HEADS):
            rows = slice(h * HEADDIM, (h + 1) * HEADDIM)
            state[rows, :] = passing[h : h + 1, :] * state[rows, :] + gained[rows, :]


def forward_scan(values, wr, delta, heads, docs, incoming):
    n, _, length = values.shape
    chunks = length // CH
    return pl.pallas_call(
        forward_kernel,
        grid=(n,),
        in_specs=[
            piece(INNER, length),
            pl.BlockSpec((1, length, STATE), lambda i: (i, 0, 0)),
            pl.BlockSpec((1, length, STATE), lambda i: (i, 0, 1)),
            piece(HP, length),
            whole(heads.shape),
            piece(*docs.shape[1:]),
            piece(INNER, STATE),
        ],
        out_specs=[piece(INNER, length), piece(chunks, INNER, STATE)],
        scratch_shapes=[
            pltpu.VMEM((INNER, STATE), F32),
            pltpu.VMEM((INNER, CH), F32),
            pltpu.VMEM((INNER, CH), BF16),
        ],
        out_shape=[
            jax.ShapeDtypeStruct((n, INNER, length), F32),
            jax.ShapeDtypeStruct((n, chunks, INNER, STATE), BF16),
        ],
        compiler_params=params(("arbitrary",)),
        name="forward_scan",
    )(values, wr, wr, delta, heads, docs, incoming)


def backward_kernel(
    val_ref, w_ref, r_ref, delta_ref, draw_ref, heads_ref, docs_ref, gy_ref, first_ref,
    start_ref, in_ref, final_ref, dsilu_ref, conv_ref, near_ref,
    gval_ref, gwr_ref, gdraw_ref, gheads_ref, ghalo_ref,
    grad, link, off, fresh, faded, gdelta, paid, sums,
):
    n, step = pl.program_id(0), pl.program_id(1)
    rate = column(heads_ref, RATE)

    @pl.when(step == 0)
    def _():
        grad[...] = in_ref[0].astype(F32)
        product = in_ref[0].astype(F32) * final_ref[0].astype(F32)
        by_head = jnp.sum(product.reshape(HEADS, HEADDIM, STATE), axis=1)
        link[0:HEADS, :] = jnp.sum(by_head, axis=1, keepdims=True)
        link[HEADS:, :] = jnp.zeros((HP - HEADS, 1), F32)

    @pl.when((n == 0) & (step == 0))
    def _():
        sums[...] = jnp.zeros_like(sums)

    writers, readers = w_ref[0], r_ref[0]
    delta = delta_ref[0]
    decay, totals, fade, to_end, passing, barred, reach = chunk_terms(delta, rate, docs_ref[0])
    columns = totals.T
    scores = nt(writers, readers)
    low_grad = grad[...].astype(BF16)
    off[...] = nt(low_grad, writers)
    gscores = jnp.zeros((CH, CH), F32)
    gdelta[HEADS:, :] = jnp.zeros((HP - HEADS, CH), F32)
    paid[HEADS:, :] = jnp.zeros((HP - HEADS, CH), F32)
    for h in range(HEADS):
        rows = slice(h * HEADDIM, (h + 1) * HEADDIM)
        spread = jnp.exp(totals[h : h + 1, :] - columns[:, h : h + 1] + barred)
        values = val_ref[0, rows, :].astype(F32)
        gy = gy_ref[0, rows, :]
        gy32 = gy.astype(F32)
        scaled = values * delta[h : h + 1, :]
        fresh[rows, :] = (scaled * to_end[h : h + 1, :]).astype(BF16)
        faded[rows, :] = (gy32 * fade[h : h + 1, :]).astype(BF16)
        gscaled = nt(gy, (spread * scores).astype(BF16)) + off[rows, :] * to_end[h : h + 1, :]
        low = scaled.astype(BF16)
        gscores = gscores + tn(low, gy) * spread
        paid[h : h + 1, :] = jnp.sum(low.astype(F32) * gscaled, axis=0, keepdims=True)
        gdelta[h : h + 1, :] = jnp.sum(values * gscaled, axis=0, keepdims=True)
        gval_ref[0, rows, :] = (
            gscaled * delta[h : h + 1, :] + gy32 * heads_ref[SKIP : SKIP + 1, h : h + 1]
        ).astype(BF16)
    low_scores = gscores.astype(BF16)
    gwr_ref[0, :, :STATE] = nn(low_scores, readers) + tn(fresh[...], low_grad)
    gwr_ref[0, :, STATE:] = tn(low_scores, writers) + tn(faded[...], start_ref[0, 0])
    off[:, :STATE] = nn(faded[...], readers)
    for h in range(HEADS):
        rows = slice(h * HEADDIM, (h + 1) * HEADDIM)
        grad[rows, :] = passing[h : h + 1, :] * grad[rows, :] + off[rows, :STATE]
    following = jnp.where(docs_ref[0, 0:1, :] == docs_ref[0, 1:2, CH - 1 :], 1.0, 0.0)
    gdecay = nn_high(first_ref[0] - paid[...], reach) + following * link[...]
    link[...] = gdecay[:, :1]
    gtotal = gdelta[...] - jnp.exp(rate) * gdecay
    gdraw = gtotal * sigmoid(draw_ref[0])
    gdraw_ref[0] = gdraw
    sums[0] += gdraw
    sums[1] += gdecay * decay

    @pl.when(step == pl.num_programs(1) - 1)
    def _():
        taps = conv_ref[...]
        near = [
            square_of(
                jnp.where(near_ref[0, j : j + 1, :] == near_ref[0, 0:1, :], 1.0, 0.0)
            )[120:, :]
            for j in range(CONV)
        ]
        for c in range(XBC // 128):
            cols = slice(c * 128, (c + 1) * 128)
            if c < INNER // 128:
                here = gval_ref[0, cols, :].astype(F32).T[:8, :]
            else:
                here = gwr_ref[0, 0:8, c * 128 - INNER : c * 128 - INNER + 128]
            pre = here * dsilu_ref[0, 0:8, cols].astype(F32)
            wide = jnp.concatenate([jnp.zeros((8, 128), F32), pre], axis=0)
            total = jnp.zeros((8, 128), F32)
            for j in range(1, CONV):
                total = total + taps[3 - j : 4 - j, cols] * wide[j : j + 8] * near[j]
            ghalo_ref[0, :, cols] = total

    @pl.when((n == pl.num_programs(0) - 1) & (step == pl.num_programs(1) - 1))
    def _():
        for i in range(2):
            both = jnp.concatenate([sums[i], jnp.zeros((128 - HP, CH), F32)], axis=0)
            gheads_ref[i : i + 1, :] = jnp.sum(both.T, axis=0, keepdims=True)
        gheads_ref[2:, :] = jnp.zeros((6, 128), F32)


def backward_scan(
    values, wr, delta, draw, heads, docs, gy, first, starts, incoming, final, dsilu, conv
):
    n, _, length = values.shape
    chunks = length // CH
    back = lambda k: chunks - 1 - k
    lanes = lambda rows: pl.BlockSpec((1, rows, CH), lambda i, k: (i, 0, back(k)))
    return pl.pallas_call(
        backward_kernel,
        grid=(n, chunks),
        in_specs=[
            lanes(INNER),
            pl.BlockSpec((1, CH, STATE), lambda i, k: (i, back(k), 0)),
            pl.BlockSpec((1, CH, STATE), lambda i, k: (i, back(k), 1)),
            lanes(HP),
            lanes(HP),
            whole(heads.shape, 2),
            pl.BlockSpec((1, 8, CH), lambda i, k: (i, 0, back(k) + LEAD // CH)),
            lanes(INNER),
            lanes(HP),
            pl.BlockSpec((1, 1, INNER, STATE), lambda i, k: (i, back(k), 0, 0)),
            pl.BlockSpec((1, INNER, STATE), lambda i, k: (i, 0, 0)),
            pl.BlockSpec((1, INNER, STATE), lambda i, k: (i, 0, 0)),
            pl.BlockSpec((1, 16, XBC), lambda i, k: (i, 0, 0)),
            whole(conv.shape, 2),
            pl.BlockSpec((1, 8, 128), lambda i, k: (i, 0, 0)),
        ],
        out_specs=[
            lanes(INNER),
            pl.BlockSpec((1, CH, 2 * STATE), lambda i, k: (i, back(k), 0)),
            lanes(HP),
            pl.BlockSpec((8, 128), lambda i, k: (0, 0)),
            pl.BlockSpec((1, 8, XBC), lambda i, k: (i, 0, 0)),
        ],
        scratch_shapes=[
            pltpu.VMEM((INNER, STATE), F32),
            pltpu.VMEM((HP, 1), F32),
            pltpu.VMEM((INNER, CH), F32),
            pltpu.VMEM((INNER, CH), BF16),
            pltpu.VMEM((INNER, CH), BF16),
            pltpu.VMEM((HP, CH), F32),
            pltpu.VMEM((HP, CH), F32),
            pltpu.VMEM((2, HP, CH), F32),
        ],
        out_shape=[
            jax.ShapeDtypeStruct((n, INNER, length), BF16),
            jax.ShapeDtypeStruct((n, length, 2 * STATE), F32),
            jax.ShapeDtypeStruct((n, HP, length), F32),
            jax.ShapeDtypeStruct((8, 128), F32),
            jax.ShapeDtypeStruct((n, 8, XBC), F32),
        ],
        compiler_params=params(("arbitrary", "arbitrary")),
        name="backward_scan",
    )(
        values, wr, wr, delta, draw, heads, docs, gy, first, starts, incoming, final, dsilu,
        conv, docs,
    )


def leave_kernel(group, packed, *refs):
    if packed:
        weights_ref, *refs = refs
        *refs, wgate_ref, wout_ref, loaded = refs
    else:
        wgate_ref, wout_ref, *refs = refs
    (
        normed_ref, turned_ref, cot_ref, tok_ref, y_ref, val_ref, r_ref, gain_ref, delta_ref,
        heads_ref, docs_ref,
        out_ref, gy_ref, gnorm_ref, first_ref, gstate_ref, grads_ref, ggain_ref, gskip_ref,
        gate, gated, upward, lifted, faded, flat, total_out, total_gate, products, skips, gains,
        wide_gain, fade, total_state,
    ) = refs
    n, k = pl.program_id(0), pl.program_id(1)
    begin = (n == 0) & (k == 0)
    end = (n == pl.num_programs(0) - 1) & (k == pl.num_programs(1) - 1)
    length = delta_ref.shape[2]
    rows_out, rows_in = INNER // group, D // group
    tiles = INNER // TILE
    lanes = range(0, ROWS, 128)
    down = lambda s: jnp.sum(s, axis=0, keepdims=True)

    def fold(v):
        return jnp.sum(v.reshape(v.shape[0] // 8, 8, 128), axis=0)

    def loads():
        copies = []
        for p in range(group):
            for q, ref, at, left in (
                (2, wgate_ref, p * rows_in, 0), (3, wgate_ref, p * rows_in, D),
                (0, wout_ref, p * rows_out, 0), (1, wout_ref, p * rows_out + rows_in, 0),
            ):
                copies.append(
                    pltpu.make_async_copy(
                        weights_ref.at[p, q],
                        ref.at[pl.ds(at, rows_in), pl.ds(left, D)],
                        loaded.at[len(copies)],
                    )
                )
        return copies

    @pl.when(begin)
    def _():
        if packed:
            for copy in loads():
                copy.start()
        total_out[...] = jnp.zeros_like(total_out)
        total_gate[...] = jnp.zeros_like(total_gate)
        skips[...] = jnp.zeros_like(skips)
        gains[...] = jnp.zeros_like(gains)
        for q in range(INNER // 128):
            wide_gain[q * 128 : (q + 1) * 128, :] = square_of(gain_ref[q : q + 1, :])

    @pl.when(k == 0)
    def _():
        own = docs_ref[0, 0:1, LEAD:]
        before = docs_ref[0, BEFORE + 1 : BEFORE + 2, LEAD : LEAD + 1]
        totals = nn_high(-jnp.exp(column(heads_ref, RATE)) * delta_ref[0], triangle(length))
        fade[...] = jnp.exp(totals) * jnp.where(own == before, 1.0, 0.0)
        total_state[...] = jnp.zeros_like(total_state)

    if packed:

        @pl.when(begin)
        def _():
            for copy in loads():
                copy.wait()

    here = pl.ds(pl.multiple_of(k * ROWS, ROWS), ROWS)

    def span(c):
        return slice(c * TILE, (c + 1) * TILE)

    def head_rows(h):
        return slice(h * HEADDIM, (h + 1) * HEADDIM)

    def open_tile(c):
        if c < tiles:
            gate[span(c), :] = nn(normed_ref[0], wgate_ref[:, span(c)]).T.astype(BF16)
            upward[span(c), :] = nt(wout_ref[span(c), :], cot_ref[0])

    squares = [jnp.zeros((8, 128), F32) for _ in lanes]
    dots = [jnp.zeros((8, 128), F32) for _ in lanes]
    open_tile(0)
    for c in range(tiles):
        open_tile(c + 1)
        for h in range(c * 4, c * 4 + 4):
            rows = head_rows(h)
            skip = heads_ref[SKIP : SKIP + 1, h : h + 1]
            gain = wide_gain[rows, :]
            for i, b in enumerate(lanes):
                g = gate[rows, b : b + 128].astype(F32)
                values = val_ref[0, rows, b : b + 128].astype(F32)
                v = (y_ref[0, rows, b : b + 128] + skip * values) * (g * sigmoid(g))
                gated[rows, b : b + 128] = v
                squares[i] = squares[i] + fold(v * v)
                dots[i] = dots[i] + fold(upward[rows, b : b + 128] * gain * v)
    scale = [lax.rsqrt(down(s) * (1.0 / INNER) + EPS) for s in squares]
    pull = [s * s * s * down(d) * (1.0 / INNER) for s, d in zip(scale, dots)]

    def close_tile(c):
        low = lifted[span(c), :]
        flat[:, span(c)] = low.T
        total_out[span(c), :] += nn(low, cot_ref[0])
        total_gate[:, span(c)] += nt(turned_ref[0], gate[span(c), :])
        total_state[span(c), :] += nn(faded[c % 2], r_ref[0])

    for c in range(tiles):
        if c > 0:
            close_tile(c - 1)
        for h in range(c * 4, c * 4 + 4):
            eight = slice(h * 8, h * 8 + 8)
            skip = heads_ref[SKIP : SKIP + 1, h : h + 1]
            fading = fade[h : h + 1, here]
            sums = jnp.zeros((8, 128), F32)
            product = [jnp.zeros((8, 128), F32) for _ in lanes]
            for at in range(h * HEADDIM, (h + 1) * HEADDIM, SUB):
                rows = slice(at, at + SUB)
                inner = slice(at - c * TILE, at - c * TILE + SUB)
                gain = wide_gain[rows, :]
                gain_sums = gains[rows, :]
                for i, b in enumerate(lanes):
                    v = gated[rows, b : b + 128]
                    u = upward[rows, b : b + 128]
                    normal = v * scale[i]
                    lifted[rows, b : b + 128] = (normal * gain).astype(BF16)
                    gain_sums = gain_sums + u * normal
                    gv = scale[i] * (u * gain) - pull[i] * v
                    g = gate[rows, b : b + 128].astype(F32)
                    sig = sigmoid(g)
                    silu = g * sig
                    low = (gv * silu).astype(BF16)
                    gy_ref[0, rows, b : b + 128] = low
                    gm = low.astype(F32)
                    faded[c % 2, inner, b : b + 128] = (gm * fading[:, b : b + 128]).astype(BF16)
                    values = val_ref[0, rows, b : b + 128].astype(F32)
                    sums = sums + fold(gm * values)
                    y = y_ref[0, rows, b : b + 128]
                    product[i] = product[i] + fold(gm * y)
                    gate[rows, b : b + 128] = (
                        gv * (y + skip * values) * (sig + silu * (1.0 - sig))
                    ).astype(BF16)
                gains[rows, :] = gain_sums
            for i, b in enumerate(lanes):
                products[eight, b : b + 128] = product[i]
            skips[eight, :] += sums
    close_tile(tiles - 1)
    for b in range(0, D, TILE):
        branch = nn(flat[...], wout_ref[:, b : b + TILE])
        out_ref[0, :, b : b + TILE] = (tok_ref[0, :, b : b + TILE].astype(F32) + branch).astype(BF16)
    for b in range(0, D, TILE):
        gnorm_ref[0, b : b + TILE, :] = nn(wgate_ref[b : b + TILE, :], gate[...]).astype(BF16)
    first_ref[0, 0:HEADS, :] = jnp.sum(products[...].reshape(HEADS, 8, ROWS), axis=1)
    first_ref[0, HEADS:, :] = jnp.zeros((HP - HEADS, ROWS), F32)

    @pl.when(k == pl.num_programs(1) - 1)
    def _():
        gstate_ref[0] = total_state[...].astype(BF16)

    @pl.when(end)
    def _():
        for p in range(group):
            grads_ref[p, :rows_out, :] = total_out[p * rows_out : (p + 1) * rows_out, :].astype(BF16)
            for half in range(2):
                at = rows_out + half * rows_in
                grads_ref[p, at : at + rows_in, :] = total_gate[
                    p * rows_in : (p + 1) * rows_in, half * D : (half + 1) * D
                ].astype(BF16)
        for q in range(INNER // 128):
            ggain_ref[q : q + 1, :] = down(gains[q * 128 : (q + 1) * 128, :].T)
        ggain_ref[INNER // 128 :, :] = jnp.zeros((16 - INNER // 128, 128), F32)
        by_head = jnp.sum(skips[...].reshape(HEADS, 8, 128), axis=1)
        by_head = jnp.concatenate([by_head, jnp.zeros((128 - HEADS, 128), F32)], axis=0)
        gskip_ref[0:1, :] = down(by_head.T)
        gskip_ref[1:, :] = jnp.zeros((7, 128), F32)


def leave(weights, normed, turned, cot, tokens, y, values, wr, gain, delta, heads, docs):
    n, length, _ = normed.shape
    group, _, rows_in, _ = weights.shape
    packed = rows_in % 16 == 0
    if packed:
        weights, loaded = [weights], [pl.BlockSpec(memory_space=pl.ANY)]
        scratch = [
            pltpu.VMEM((D, INNER), BF16),
            pltpu.VMEM((INNER, D), BF16),
            pltpu.SemaphoreType.DMA((4 * group,)),
        ]
    else:
        gate = jnp.concatenate([weights[:, 2], weights[:, 3]], axis=-1).reshape(D, INNER)
        weights = [gate, weights[:, :2].reshape(INNER, D)]
        loaded, scratch = [whole(a.shape, 2) for a in weights], []
    grads = (group, 4 * rows_in, D)
    rows = lambda width: pl.BlockSpec((1, ROWS, width), lambda i, k: (i, k, 0))
    lanes = lambda height: pl.BlockSpec((1, height, ROWS), lambda i, k: (i, 0, k))
    each = lambda *shape: pl.BlockSpec((1,) + shape, lambda i, k: (i, 0, 0))
    return pl.pallas_call(
        partial(leave_kernel, group, packed),
        grid=(n, length // ROWS),
        in_specs=loaded + [
            rows(D), lanes(D), rows(D), rows(D), lanes(INNER), lanes(INNER),
            pl.BlockSpec((1, ROWS, STATE), lambda i, k: (i, k, 1)),
            whole(gain.shape, 2), each(HP, length), whole(heads.shape, 2), each(*docs.shape[1:]),
        ],
        out_specs=[
            rows(D), lanes(INNER), lanes(D), lanes(HP), each(INNER, STATE), whole(grads, 2),
            whole((16, 128), 2), whole((8, 128), 2),
        ],
        scratch_shapes=[
            pltpu.VMEM((INNER, ROWS), BF16),
            pltpu.VMEM((INNER, ROWS), F32),
            pltpu.VMEM((INNER, ROWS), F32),
            pltpu.VMEM((INNER, ROWS), BF16),
            pltpu.VMEM((2, TILE, ROWS), BF16),
            pltpu.VMEM((ROWS, INNER), BF16),
            pltpu.VMEM((INNER, D), F32),
            pltpu.VMEM((D, INNER), F32),
            pltpu.VMEM((HEADS * 8, ROWS), F32),
            pltpu.VMEM((HEADS * 8, 128), F32),
            pltpu.VMEM((INNER, 128), F32),
            pltpu.VMEM((INNER, 128), F32),
            pltpu.VMEM((HP, length), F32),
            pltpu.VMEM((INNER, STATE), F32),
        ] + scratch,
        out_shape=[
            jax.ShapeDtypeStruct((n, length, D), BF16),
            jax.ShapeDtypeStruct((n, INNER, length), BF16),
            jax.ShapeDtypeStruct((n, D, length), BF16),
            jax.ShapeDtypeStruct((n, HP, length), F32),
            jax.ShapeDtypeStruct((n, INNER, STATE), BF16),
            jax.ShapeDtypeStruct(grads, BF16),
            jax.ShapeDtypeStruct((16, 128), F32),
            jax.ShapeDtypeStruct((8, 128), F32),
        ],
        compiler_params=params(("arbitrary", "arbitrary")),
        name="leave",
    )(*weights, normed, turned, cot, tokens, y, values, wr, gain, delta, heads, docs)


def exit_kernel(
    gval_ref, gwr_ref, dsilu_ref, raw_ref, docs_ref, conv_ref, back_ref, normed_ref, turned_ref,
    wraw_ref, gdraw_ref, dlow_ref, gnorm_ref, tok_ref, cot_ref, gain_ref,
    grad_ref, graw_ref, gdelta_ref, ggain_ref, gconv_ref,
    pre, low_pre, moved, halo_terms, shift, low, lifted, total, sums,
):
    n = pl.program_id(0)
    length = dsilu_ref.shape[1]
    last = n == pl.num_programs(0) - 1

    @pl.when(n == 0)
    def _():
        total[...] = jnp.zeros_like(total)
        sums[...] = jnp.zeros_like(sums)
        gdelta_ref[...] = jnp.zeros_like(gdelta_ref)
        ggain_ref[...] = jnp.zeros_like(ggain_ref)

    def shifts(rows, extent, near):
        first = lax.broadcasted_iota(jnp.int32, (rows, extent), 0)
        second = lax.broadcasted_iota(jnp.int32, (rows, extent), 1)
        return [
            jnp.where(second == first + j, near[j - 1], 0.0).astype(BF16) for j in range(1, CONV)
        ]

    near = [
        jnp.where(docs_ref[0, j : j + 1, :] == docs_ref[0, 0:1, :], 1.0, 0.0)
        for j in range(1, CONV)
    ]
    for i in range(length // 128):
        square = [square_of(v[:, LEAD + i * 128 : LEAD + i * 128 + 128]) for v in near]
        square = [jnp.concatenate([v, v[:, : SPAN - 128]], axis=1) for v in square]
        shift[i] = jnp.concatenate(shifts(128, SPAN, square), axis=0)
    square = [square_of(v[:, LEAD - 128 : LEAD])[128 - HALO :, : 2 * HALO] for v in near]
    ahead = jnp.concatenate(shifts(HALO, 2 * HALO, square), axis=0)
    for slot in range(2):
        low_pre[slot, :HALO, :] = jnp.zeros((HALO, TILE), BF16)
        low_pre[slot, HALO + length :, :] = jnp.zeros((HALO, TILE), BF16)
    tiles = XBC // TILE
    blocks = length // 128

    def span_of(c):
        return slice(c * TILE, (c + 1) * TILE)

    def open_tile(c):
        if c == tiles:
            return
        if c < INNER // TILE:
            here = gval_ref[0, span_of(c), :].astype(F32).T
        else:
            here = gwr_ref[0]
        here = here * dsilu_ref[0, :, span_of(c)].astype(F32)
        pre[c % 2] = here
        low_pre[c % 2, HALO : HALO + length, :] = here.astype(BF16)
        halo_terms[c % 2] = nn(ahead, low_pre[c % 2, : 2 * HALO, :])
        for i in range(blocks):
            moved[c % 2 * blocks + i] = nn(
                shift[i], low_pre[c % 2, HALO + i * 128 : HALO + i * 128 + SPAN, :]
            )

    def close_tile(c):
        total[:, span_of(c)] += nn(turned_ref[0], low[c % 2])
        through = nt(low[c % 2], wraw_ref[:, span_of(c)])
        if c == 0:
            lifted[...] = through
        else:
            lifted[...] += through

    def fold(v):
        return jnp.sum(v.reshape(v.shape[0] // 8, 8, 128), axis=0)

    open_tile(0)
    for c in range(tiles):
        slot = c % 2
        open_tile(c + 1)
        if c > 0:
            close_tile(c - 1)
        for half in range(0, TILE, 128):
            cols = slice(half, half + 128)
            wide = slice(c * TILE + half, c * TILE + half + 128)
            w = conv_ref[:, wide]
            folded = [sums[k, :, wide] for k in range(CONV + 1)]
            raw = raw_ref[0, :HALO, wide].astype(F32)
            for j in range(1, CONV):
                term = halo_terms[slot, (j - 1) * HALO : j * HALO, cols]
                folded[3 - j] = folded[3 - j] + fold(raw * term)
            for b in range(0, length, 64):
                raw = raw_ref[0, HALO + b : HALO + b + 64, wide].astype(F32)
                now = pre[slot, b : b + 64, cols]
                grad = w[3:4] * now
                folded[3] = folded[3] + fold(raw * now)
                folded[4] = folded[4] + fold(now)
                for j in range(1, CONV):
                    at = (j - 1) * 128 + b % 128
                    term = moved[slot * blocks + b // 128, at : at + 64, cols]
                    grad = grad + w[3 - j : 4 - j] * term
                    folded[3 - j] = folded[3 - j] + fold(raw * term)
                if b == length - 64:
                    grad = jnp.concatenate([grad[:56], grad[56:] + back_ref[0, :, wide]], axis=0)
                low[slot, b : b + 64, cols] = grad.astype(BF16)
            for k in range(CONV + 1):
                sums[k, :, wide] = folded[k]
    close_tile(tiles - 1)

    gdraw = gdraw_ref[0].astype(BF16)
    gdelta_ref[...] += nn(gdraw, normed_ref[0])
    gain = gain_ref[...]
    gains = jnp.zeros((8, D), F32)
    for b in range(0, length, 128):
        rows = slice(b, b + 128)
        up = lifted[rows, :] + gnorm_ref[0, :, rows].astype(F32).T + tn(gdraw[:, rows], dlow_ref[...])
        x = tok_ref[0, rows, :].astype(F32)
        scale = lax.rsqrt(jnp.mean(x * x, axis=-1, keepdims=True) + EPS)
        normal = x * scale
        gains = gains + jnp.sum((up * normal).reshape(16, 8, D), axis=0)
        up = up * gain
        inner = jnp.mean(up * normal, axis=-1, keepdims=True)
        grad = cot_ref[0, rows, :].astype(F32) + scale * (up - normal * inner)
        grad_ref[0, rows, :] = grad.astype(BF16)
    ggain_ref[0:1, :] += jnp.sum(gains, axis=0, keepdims=True)

    @pl.when(last)
    def _():
        graw_ref[...] = total[...].astype(BF16)
        gconv_ref[0 : CONV + 1, :] = jnp.sum(sums[...], axis=1)


def leave_back(
    gval, gwr, dsilu, raw, docs, conv, back, normed, turned, wraw, gdraw, dlow, gnorm, tokens,
    cotangent, gain,
):
    n, length, _ = dsilu.shape
    return pl.pallas_call(
        exit_kernel,
        grid=(n,),
        in_specs=[
            piece(INNER, length), piece(length, 2 * STATE), piece(length, XBC),
            piece(length + HALO, XBC), piece(*docs.shape[1:]), whole(conv.shape), piece(8, XBC),
            piece(length, D), piece(D, length), whole(wraw.shape), piece(HP, length),
            whole(dlow.shape), piece(D, length), piece(length, D), piece(length, D),
            whole(gain.shape),
        ],
        out_specs=[
            piece(length, D), whole((D, XBC)), whole((HP, D)), whole((8, D)), whole((8, XBC)),
        ],
        out_shape=[
            jax.ShapeDtypeStruct((n, length, D), BF16),
            jax.ShapeDtypeStruct((D, XBC), BF16),
            jax.ShapeDtypeStruct((HP, D), F32),
            jax.ShapeDtypeStruct((8, D), F32),
            jax.ShapeDtypeStruct((8, XBC), F32),
        ],
        scratch_shapes=[
            pltpu.VMEM((2, length, TILE), F32),
            pltpu.VMEM((2, length + 2 * HALO, TILE), BF16),
            pltpu.VMEM((2 * (length // 128), (CONV - 1) * 128, TILE), F32),
            pltpu.VMEM((2, (CONV - 1) * HALO, TILE), F32),
            pltpu.VMEM((length // 128, (CONV - 1) * 128, SPAN), BF16),
            pltpu.VMEM((2, length, TILE), BF16),
            pltpu.VMEM((length, D), F32),
            pltpu.VMEM((D, XBC), F32),
            pltpu.VMEM((CONV + 1, 8, XBC), F32),
        ],
        compiler_params=params(("arbitrary",)),
        name="leave_back",
    )(
        gval, gwr, dsilu, raw, docs, conv, back, normed, turned, wraw, gdraw, dlow, gnorm, tokens,
        cotangent, gain,
    )


def tiles_of(extent):
    return -(-extent // 128)


def pieces_of(rows):
    return [(i, i * 128, min(128, rows - i * 128)) for i in range(tiles_of(rows))]


def split_three(v):
    high = v.astype(BF16)
    rest = v - high.astype(F32)
    middle = rest.astype(BF16)
    low = (rest - middle.astype(F32)).astype(BF16)
    return jnp.concatenate([high, middle, low], axis=0)


def join_three(v):
    return v[0:8] + v[8:16] + v[16:24]


def inverse_factor(gram):
    rows = lax.broadcasted_iota(jnp.int32, (8, 8), 0)
    cols = lax.broadcasted_iota(jnp.int32, (8, 8), 1)
    left, right = gram, jnp.where(rows == cols, 1.0, 0.0)
    for j in range(7):
        factor = jnp.where(rows[:, :1] > j, left[:, j : j + 1] / left[j : j + 1, j : j + 1], 0.0)
        left, right = left - factor * left[j : j + 1, :], right - factor * right[j : j + 1, :]
    pivots = jnp.sum(jnp.where(rows == cols, left, 0.0), axis=1, keepdims=True)
    return right * lax.rsqrt(pivots)


RIGHT_OUT = PROJ // 128
DELTA = RIGHT_OUT + D // 128
REST = DELTA + HEADS // 8 * (D // 128)
REST_ROWS = D // 128 + (CONV + 1) * (XBC // 128) + INNER // 128 + 3
SUMMED = REST + -(-REST_ROWS // 8)


class Scatter:
    def __init__(self, group, x_ref, from_core, pairs, from_far, joint, send, recv):
        self.nf = group // 2
        self.x_ref, self.from_core, self.pairs, self.from_far = x_ref, from_core, pairs, from_far
        self.joint, self.send, self.recv = joint, send, recv
        self.r, self.f, self.s = (lax.axis_index(name) for name in ("rep", "fsdp", "seq"))
        self.copies = []
        half = x_ref.shape[1] // 2
        self.parts = [slice(0, half), slice(half, 2 * half)]
        f = self.f
        if self.nf == 4:
            x, y = f + 1 - 2 * lax.rem(f, 2), lax.rem(f + 2, 4)
            self.order = [lax.rem(x + 2, 4), x, y, f]
        else:
            self.order = [lax.rem(f + 1 + j, self.nf) for j in range(self.nf)]

    def start(self, src, dst, device):
        k = len(self.copies)
        copy = pltpu.make_async_remote_copy(
            src, dst, self.send.at[k], self.recv.at[k], device_id=device, device_id_type=MESH
        )
        copy.start()
        self.copies.append(copy)
        return copy

    def begin(self):
        other = (self.r, self.f, 1 - self.s)
        self.near = [
            self.start(self.x_ref.at[f * 2 + 1 - self.s], self.from_core.at[j], other)
            for j, f in enumerate(self.order)
        ]

    def device(self, j):
        return (self.r, self.order[j], self.s)

    def cross(self):
        self.far = []
        for j, f in enumerate(self.order):
            self.near[j].wait_recv()
            total = self.x_ref[f * 2 + self.s].astype(F32) + self.from_core[j].astype(F32)
            self.pairs[j] = total.astype(BF16)
            if self.nf != 4 and j < self.nf - 1:
                self.far.append(self.start(self.pairs.at[j], self.from_far.at[j], self.device(j)))
            if self.nf == 4 and j < 3:
                for half, part in enumerate(self.parts):
                    if j == 0 or half == j - 1:
                        to = half + 1 if j == 0 else j
                        self.far.append(
                            self.start(
                                self.pairs.at[j, part], self.from_far.at[j, part], self.device(to)
                            )
                        )

    def turn(self):
        if self.nf != 4:
            return
        for half, part in enumerate(self.parts):
            self.far[half].wait_recv()
            to = 2 - half
            total = self.pairs[to, part].astype(F32) + self.from_far[0, part].astype(F32)
            self.joint[half] = total.astype(BF16)
            self.far.append(
                self.start(self.joint.at[half], self.from_far.at[to, part], self.device(to))
            )

    def end(self, o_ref):
        if self.nf == 4:
            for copy in self.far[2:]:
                copy.wait_recv()
            total = self.pairs[3].astype(F32)
            for j in (1, 2):
                total = total + self.from_far[j].astype(F32)
        else:
            total = self.pairs[self.nf - 1].astype(F32)
            for j, copy in enumerate(self.far):
                copy.wait_recv()
                total = total + self.from_far[j].astype(F32)
        o_ref[...] = total
        for copy in self.copies:
            copy.wait_send()


class Exchange:
    def __init__(self, group, replicas):
        self.group, self.replicas = group, replicas
        r, f, s = lax.axis_index("rep"), lax.axis_index("fsdp"), lax.axis_index("seq")
        self.r, self.me = r, f * 2 + s
        self.peers = []
        for j in range(1, group):
            p = lax.rem(self.me + j, group)
            self.peers.append((p, (r, lax.div(p, 2), lax.rem(p, 2))))
        self.others = [(lax.rem(r + j, replicas), f, s) for j in range(1, replicas)]

    def greet(self):
        barrier = pltpu.get_barrier_semaphore()
        for device in [d for _, d in self.peers] + self.others:
            pl.semaphore_signal(barrier, inc=1, device_id=device, device_id_type=MESH)

    def met(self):
        pl.semaphore_wait(pltpu.get_barrier_semaphore(), self.group + self.replicas - 2)

    def sum(self, x_ref, o_ref, own, from_group, from_reps, send, recv, second=None, third=None):
        group, replicas, me = self.group, self.replicas, self.me
        width = own.shape[0]
        copies = []

        def start(src, dst, device):
            k = len(copies)
            copy = pltpu.make_async_remote_copy(
                src, dst, send.at[k], recv.at[k], device_id=device, device_id_type=MESH
            )
            copy.start()
            copies.append(copy)
            return copy

        arriving = [
            start(x_ref.at[pl.ds(p * width, width)], from_group.at[j], device)
            for j, (p, device) in enumerate(self.peers)
        ]
        total = x_ref[pl.ds(me * width, width)]
        for j, copy in enumerate(arriving):
            copy.wait_recv()
            total = total + from_group[j]
        own[...] = total
        from_reps[pl.ds(self.r, 1)] = total[None]
        arriving = [start(own, from_reps.at[self.r], device) for device in self.others]
        if second is not None:
            second()
        for copy in arriving:
            copy.wait_recv()
        total = from_reps[0]
        for j in range(1, replicas):
            total = total + from_reps[j]
        mine = pl.ds(me * width, width)
        o_ref[mine] = total
        arriving = [start(o_ref.at[mine], o_ref.at[mine], device) for _, device in self.peers]
        if third is not None:
            third()
        for copy in arriving:
            copy.wait_recv()
        for copy in copies:
            copy.wait_send()


def compress_kernel(
    group, replicas,
    sin_ref, sout_ref, grads_ref, raw_ref, ein_ref, eout_ref, gdelta_ref, ggain_ref,
    gconv_ref, ggate_ref, gheads_ref, gskip_ref,
    sum_ref, left_in_ref, left_out_ref, turned_in_ref, turned_out_ref, raw_total_ref,
    lefts, left_sums, hat, rights,
    own_a, group_a, reps_a, own_b, group_b, reps_b, send_a, recv_a, send_b, recv_b,
    from_core, pairs, from_far, joint, send_c, recv_c, held_raw, held_grads, held_in, held_out,
    split_in, split_out, load,
):
    rows_in, rows_out = ein_ref.shape[0], eout_ref.shape[0]
    out_part = slice(0, rows_out)
    gate_parts = [slice(rows_out + i * rows_in, rows_out + (i + 1) * rows_in) for i in range(2)]
    ahead = tiles_of(rows_in)
    width = ahead + tiles_of(rows_out)
    exchange = Exchange(group, replicas)
    exchange.greet()
    loads = [
        pltpu.make_async_copy(src, dst, load.at[k])
        for k, (src, dst) in enumerate(
            ((ein_ref, held_in), (eout_ref, held_out), (grads_ref, held_grads), (raw_ref, held_raw))
        )
    ]
    for copy in loads:
        copy.start()
    raw_ref, grads_ref = held_raw, held_grads

    lefts[...] = jnp.zeros_like(lefts)
    mine = pl.ds(exchange.me * width, width)

    def place(index, values, rows, first):
        for i, at, n in pieces_of(rows):
            lefts[index + first + i, :, :n] += values[:, at : at + n]

    def place_own(values, rows, first):
        for i, at, n in pieces_of(rows):
            part = values[:, at : at + n]
            if n < 128:
                part = jnp.concatenate([part, jnp.zeros((8, 128 - n), F32)], axis=1)
            where = pl.ds(exchange.me * width + first + i, 1)
            lefts[where] = lefts[where] + part[None]

    s_in, s_out = split_three(sin_ref[...]), split_three(sout_ref[...])
    for k, (held, split, start, rows, first) in enumerate(
        ((held_in, split_in, s_in, rows_in, 0), (held_out, split_out, s_out, rows_out, ahead))
    ):
        loads[k].wait()
        high = held[...].astype(BF16)
        split[0] = high
        split[1] = (held[...] - high.astype(F32)).astype(BF16)
        place_own(join_three(nt(start, split[0]) + nt(start, split[1])), rows, first)
    loads[2].wait()
    for p in range(group):
        product = nt(s_in[:, :D], grads_ref[p, gate_parts[0]])
        product = product + nt(s_in[:, D:INNER], grads_ref[p, gate_parts[1]])
        place(p * width, join_three(product), rows_in, 0)
        place(p * width, join_three(nt(s_out, grads_ref[p, out_part])), rows_out, ahead)
    loads[3].wait()
    exchange.met()
    scatter = Scatter(group, raw_ref, from_core, pairs, from_far, joint, send_c, recv_c)
    scatter.begin()
    for p in range(group):
        place(p * width, join_three(nt(s_in[:, INNER:], raw_ref[p])), rows_in, 0)
    exchange.sum(
        lefts, left_sums, own_a, group_a, reps_a, send_a, recv_a, scatter.cross, scatter.turn
    )

    for first, last in ((0, ahead), (ahead, width)):
        gram = jnp.zeros((8, 8), F32)
        for p in range(group):
            for i in range(first, last):
                tile = left_sums[p * width + i] * (1.0 / replicas)
                gram = gram + nt_high(tile, tile)
        inverse = inverse_factor(gram)
        for p in range(group):
            for i in range(first, last):
                hat[p * width + i] = nn_high(inverse, left_sums[p * width + i] * (1.0 / replicas))
    own = hat[mine]
    for first, rows, left_ref, turned_ref in (
        (0, rows_in, left_in_ref, turned_in_ref), (ahead, rows_out, left_out_ref, turned_out_ref)
    ):
        for i, at, n in pieces_of(rows):
            turned_ref[:, at : at + n] = own[first + i][:, :n]
            left_ref[at : at + n, :] = own[first + i].T[:n, :]

    def joined(tiles, start, rows):
        return jnp.concatenate([tiles[start + i][:, :n] for i, _, n in pieces_of(rows)], axis=1)

    def product(matrices, rows, skipped, error, at):
        spread = [split_three(joined(hat, p * width + skipped, rows)) for p in range(group)]
        mixed = split_three(joined(own, skipped, rows))
        columns = 0
        for ref, part, extent in matrices:
            for b in range(0, extent, TILE):
                total = nn(spread[0], ref[0, part, b : b + TILE])
                for p in range(1, group):
                    total = total + nn(spread[p], ref[p, part, b : b + TILE])
                here = columns + b
                total = total + nn(mixed, error[0, :, here : here + TILE])
                total = total + nn(mixed, error[1, :, here : here + TILE])
                right = join_three(total)
                for half in range(0, TILE, 128):
                    rights[at + (here + half) // 128] = right[:, half : half + 128]
            columns += extent

    every = slice(0, rows_in)
    product(
        [(grads_ref, part, D) for part in gate_parts] + [(raw_ref, every, XBC)],
        rows_in, 0, split_in, 0,
    )
    product([(grads_ref, out_part, D)], rows_out, ahead, split_out, RIGHT_OUT)
    for g in range(HEADS // 8):
        for q in range(D // 128):
            rights[DELTA + g * (D // 128) + q] = gdelta_ref[
                g * 8 : g * 8 + 8, q * 128 : q * 128 + 128
            ]
    rights[REST:] = jnp.zeros((rights.shape[0] - REST, 8, 128), F32)
    rest = [ggain_ref[0:1, q * 128 : q * 128 + 128] for q in range(D // 128)]
    for k in range(CONV + 1):
        rest += [gconv_ref[k : k + 1, q * 128 : q * 128 + 128] for q in range(XBC // 128)]
    rest += [ggate_ref[q : q + 1, :] for q in range(INNER // 128)]
    rest += [gheads_ref[0:1, :], gheads_ref[1:2, :], gskip_ref[0:1, :]]
    for i in range(0, REST_ROWS, 8):
        eight = rest[i : i + 8]
        rights[REST + i // 8, : len(eight), :] = jnp.concatenate(eight, axis=0)
    exchange.sum(rights, sum_ref, own_b, group_b, reps_b, send_b, recv_b)
    scatter.end(raw_total_ref)


def compress(starts, grads, raw, errors, smalls):
    group = grads.shape[0]
    replicas = lax.axis_size("rep")
    raw = raw.reshape(group, D // group, XBC)
    rows_in, rows_out = errors[0].shape[0], errors[1].shape[0]
    width = tiles_of(rows_in) + tiles_of(rows_out)
    block = (rows_in, XBC)
    share = -(-SUMMED // group)
    dma = pltpu.SemaphoreType.DMA((2 * (group - 1) + replicas - 1,))
    tiles = lambda *n: pltpu.VMEM(n + (8, 128), F32)
    vmem = pl.BlockSpec(memory_space=pltpu.VMEM)
    arrays = [*starts, grads, raw, *errors, *smalls]
    return pl.pallas_call(
        partial(compress_kernel, group, replicas),
        out_shape=[
            jax.ShapeDtypeStruct((group * share, 8, 128), F32),
            jax.ShapeDtypeStruct((rows_in, 8), F32),
            jax.ShapeDtypeStruct((rows_out, 8), F32),
            jax.ShapeDtypeStruct((8, rows_in), F32),
            jax.ShapeDtypeStruct((8, rows_out), F32),
            jax.ShapeDtypeStruct((rows_in, XBC), F32),
        ],
        in_specs=[vmem] * 2 + [pl.BlockSpec(memory_space=pl.ANY)] * 4 + [vmem] * len(smalls),
        out_specs=[vmem] * 6,
        scratch_shapes=[
            tiles(group * width), tiles(group * width), tiles(group * width),
            tiles(group * share),
            tiles(width), tiles(group - 1, width), tiles(replicas, width),
            tiles(share), tiles(group - 1, share), tiles(replicas, share),
            dma, dma, dma, dma,
            pltpu.VMEM((group // 2,) + block, BF16),
            pltpu.VMEM((group // 2,) + block, BF16),
            pltpu.VMEM((group // 2 - 1,) + block, BF16),
            pltpu.VMEM((2, rows_in // 2, XBC), BF16),
            pltpu.SemaphoreType.DMA((group + 2,)),
            pltpu.SemaphoreType.DMA((group + 2,)),
            pltpu.VMEM(raw.shape, BF16),
            pltpu.VMEM(grads.shape, BF16),
            pltpu.VMEM(errors[0].shape, F32),
            pltpu.VMEM(errors[1].shape, F32),
            pltpu.VMEM((2,) + errors[0].shape, BF16),
            pltpu.VMEM((2,) + errors[1].shape, BF16),
            pltpu.SemaphoreType.DMA((4,)),
        ],
        compiler_params=pltpu.CompilerParams(
            collective_id=2, has_side_effects=True, vmem_limit_bytes=VMEM_LIMIT
        ),
        name="compress",
    )(*arrays)


def finish_kernel(
    rates, replicas, rights_ref, tin_ref, tout_ref, lin_ref, lout_ref,
    win_ref, min_ref, ein_ref, raw_ref, wout_ref, mout_ref, eout_ref, out_ref, low_ref, high_ref,
    nwin_ref, nmin_ref, nein_ref, nwout_ref, nmout_ref, neout_ref,
    rin_ref, rout_ref, ntin_ref, ntout_ref,
):
    @pl.when(pl.program_id(0) == 0)
    def _():
        for ref, at, extent in ((rin_ref, 0, PROJ), (rout_ref, RIGHT_OUT, D)):
            for q in range(extent // 128):
                ref[:, q * 128 : q * 128 + 128] = rights_ref[at + q] * (1.0 / replicas)
        ntin_ref[...] = tin_ref[...]
        ntout_ref[...] = tout_ref[...]

    def update(w, m, e, nw, nm, ne, left_ref, grads, at, rate):
        rows = w.shape[0]
        left = [jnp.broadcast_to(left_ref[:, k : k + 1], (rows, 128)) for k in range(8)]
        begin = 0
        for grad in grads:
            for b in range(0, grad.shape[1], 128):
                cols = slice(begin + b, begin + b + 128)
                right = rights_ref[at + (begin + b) // 128] * (1.0 / replicas)
                approx = left[0] * right[0:1]
                for k in range(1, 8):
                    approx = approx + left[k] * right[k : k + 1]
                momentum = MOMENTUM * m[:, cols] + approx
                nm[:, cols] = momentum
                nw[:, cols] = w[:, cols] - rate * momentum
                ne[:, cols] = (grad[:, b : b + 128].astype(F32) + e[:, cols]) - approx
            begin += grad.shape[1]

    update(
        win_ref, min_ref, ein_ref, nwin_ref, nmin_ref, nein_ref, lin_ref, (low_ref, high_ref, raw_ref), 0,
        rates[0],
    )
    update(
        wout_ref, mout_ref, eout_ref, nwout_ref, nmout_ref, neout_ref, lout_ref, (out_ref,),
        RIGHT_OUT, rates[1],
    )


def finish(rates, replicas, rights, turned_in, turned_out, left_in, left_out, wide, narrow, grads):
    rows_in, rows_out = left_in.shape[0], left_out.shape[0]
    steps = 3 if rows_in % 48 == 0 else 1
    block = lambda a: pl.BlockSpec((a.shape[0] // steps, a.shape[1]), lambda i: (i, 0))
    like = lambda a: jax.ShapeDtypeStruct(a.shape, F32)
    step_in, step_out = rows_in // steps, rows_out // steps
    parts = [pl.BlockSpec((step_out, D), lambda i: (i, 0))] + [
        pl.BlockSpec((step_in, D), lambda i, k=k: ((rows_out + k * rows_in) // step_in + i, 0))
        for k in range(2)
    ]
    arrays = [*wide, *narrow]
    outs = [*wide[:3], *narrow[:3]]
    extra = [(8, PROJ), (8, D), turned_in.shape, turned_out.shape]
    return pl.pallas_call(
        partial(finish_kernel, rates, replicas),
        grid=(steps,),
        in_specs=[
            whole(rights.shape), whole(turned_in.shape), whole(turned_out.shape),
            block(left_in), block(left_out), *map(block, arrays), *parts,
        ],
        out_specs=[*map(block, outs), *map(whole, extra)],
        out_shape=[*map(like, outs), *(jax.ShapeDtypeStruct(e, F32) for e in extra)],
        compiler_params=params(("arbitrary",)),
        name="finish",
    )(rights, turned_in, turned_out, left_in, left_out, *arrays, grads, grads, grads)


def step_rates(tokens_replica):
    grad_scale = 0.3 * math.sqrt(tokens_replica)
    return (
        0.5 / (math.sqrt(D) * grad_scale),
        0.5 / (math.sqrt(INNER) * grad_scale),
        0.1 / grad_scale,
    )


def to_later(block):
    return lax.ppermute(block, "seq", [(i, i + 1) for i in range(lax.axis_size("seq") - 1)])


def to_earlier(block):
    return lax.ppermute(block, "seq", [(i + 1, i) for i in range(lax.axis_size("seq") - 1)])


def gather_rows(shard):
    return lax.all_gather(shard, ("fsdp", "seq"), axis=0, tiled=True)


def scatter_rows(total):
    return lax.psum_scatter(total, ("fsdp", "seq"), scatter_dimension=0, tiled=True)


def body(
    tokens,
    cotangent,
    segments,
    input_weight,
    output_weight,
    small_values,
    input_momentum,
    output_momentum,
    small_momentum,
    input_error,
    output_error,
    input_start,
    output_start,
):
    shape = tokens.shape
    pieces = shape[0] * shape[1]
    length = shape[2]
    replicas = lax.axis_size("rep")
    tokens_replica = pieces * length * lax.axis_size("fsdp") * lax.axis_size("seq")
    rate_in, rate_out, rate_small = step_rates(tokens_replica)

    tokens = tokens.reshape(pieces, length, D)
    cotangent = cotangent.reshape(pieces, length, D)
    small_rows = jnp.pad(small_values, (0, -small_values.shape[0] % 1024)).reshape(-1, 128)
    group = lax.axis_size("fsdp") * lax.axis_size("seq")
    weights = jnp.concatenate(
        [output_weight, input_weight[:, :D], input_weight[:, D:INNER]], axis=0
    ).astype(BF16)
    weights = gather_rows(weights).reshape(group, 4, -1, D)
    delta_rows = small_values[D:AT_CONV].reshape(D, HEADS).astype(BF16).T
    delta_rows = jnp.pad(delta_rows, ((0, HP - HEADS), (0, 0)))
    raw_full, halo, norm_gain, conv, gate_gain, heads, docs = gather_raw(
        input_weight, tokens, small_rows, segments.reshape(pieces, 1, segments.shape[2])
    )
    normed, turned, raw, dsilu, values, wr, draw, delta, send = enter(
        tokens, halo, norm_gain, raw_full, delta_rows, conv, heads, docs
    )
    y, starts = forward_scan(values, wr, delta, heads, docs, to_later(send))
    output, gy, gnorm, first, gstate, grads, ggate, gskip = leave(
        weights, normed, turned, cotangent, tokens, y, values, wr, gate_gain, delta, heads, docs
    )
    total = scatter_rows(grads.reshape(-1, D))
    gval, gwr, gdraw, gheads, ghalo = backward_scan(
        values, wr, delta, draw, heads, docs, gy, first, starts, to_earlier(gstate), send, dsilu,
        conv,
    )
    input_grad, grad_raw, gdelta, ggain, gconv = leave_back(
        gval, gwr, dsilu, raw, docs, conv, to_earlier(ghalo), normed, turned, raw_full, gdraw,
        delta_rows, gnorm, tokens, cotangent, norm_gain,
    )
    rights, left_in, left_out, turned_in, turned_out, raw_total = compress(
        (input_start.T, output_start.T),
        grads,
        grad_raw,
        (input_error[0], output_error[0]),
        (gdelta, ggain, gconv, ggate, gheads, gskip),
    )
    (
        new_input_weight, new_input_momentum, new_input_error,
        new_output_weight, new_output_momentum, new_output_error,
        input_right, output_right, input_left, output_left,
    ) = finish(
        (rate_in, rate_out), replicas, rights, turned_in, turned_out, left_in, left_out,
        (input_weight, input_momentum, input_error[0], raw_total),
        (output_weight, output_momentum, output_error[0]),
        total,
    )
    rest = rights[REST:SUMMED].reshape(-1, 128)[:REST_ROWS]
    turned_delta = rights[DELTA:REST].reshape(HEADS // 8, D // 128, 8, 128)
    small_sum = jnp.concatenate(
        [
            rest[: D // 128].reshape(-1),
            turned_delta.transpose(1, 3, 0, 2).reshape(-1),
            rest[D // 128 : -3].reshape(-1),
            rest[-3:, :HEADS].reshape(-1),
        ]
    )
    new_small_momentum = MOMENTUM * small_momentum + small_sum / replicas
    new_small_values = small_values - rate_small * new_small_momentum
    return (
        output.reshape(shape),
        input_grad.reshape(shape),
        new_input_weight,
        new_output_weight,
        new_input_momentum,
        new_output_momentum,
        new_small_values,
        new_small_momentum,
        input_left.T,
        input_right.T,
        output_left.T,
        output_right.T,
        new_input_error[None],
        new_output_error[None],
    )


def solution(mesh):
    return jax.shard_map(
        body,
        mesh=mesh,
        in_specs=(
            P(None, ("rep", "fsdp"), "seq", None),
            P(None, ("rep", "fsdp"), "seq", None),
            P(None, ("rep", "fsdp"), None),
            P(("fsdp", "seq"), None),
            P(("fsdp", "seq"), None),
            P(),
            P(("fsdp", "seq"), None),
            P(("fsdp", "seq"), None),
            P(),
            P("rep", ("fsdp", "seq"), None),
            P("rep", ("fsdp", "seq"), None),
            P(),
            P(),
        ),
        out_specs=(
            P(None, ("rep", "fsdp"), "seq", None),
            P(None, ("rep", "fsdp"), "seq", None),
            P(("fsdp", "seq"), None),
            P(("fsdp", "seq"), None),
            P(("fsdp", "seq"), None),
            P(("fsdp", "seq"), None),
            P(),
            P(),
            P(("fsdp", "seq"), None),
            P(),
            P(("fsdp", "seq"), None),
            P(),
            P("rep", ("fsdp", "seq"), None),
            P("rep", ("fsdp", "seq"), None),
        ),
        check_vma=False,
    )
```

profile of v0, /device:TPU:0, one launch (start us, length us, event | category | flops | bytes accessed | tf_op | source)
XLA Modules:
  0.0 219.7 jit_solution(536527787221431623)
XLA Ops:
  7.2 1.1 convert.12
  8.3 1.4 convert.13
  9.7 0.9 pad_maximum_fusion
  10.6 0.0 reduce-scatter.2.cloned.1.call-start
  10.7 0.3 convert_element_type.9
  11.0 0.1 copy.29
  11.1 0.6 pad.9.dlow_ref
  11.7 0.7 pad_bitcast_fusion.small_ref
  12.4 26.7 %gather_raw.1 = (bf16[8,96,1792]{2,1,0:T(8,128)(2,1)}, bf16[2,16,768]{2,1,0:T(8,128)(2,1)}, f32[1,768]{1,0:T(1,128)}, f32[5,1792]{1,0:T(8,128)}, f32[12,128]{1,0...) custom-call(f32[96,3328]{1,0:T(8,128)} %win_ref.1, bf16[2,512,768]{2,1,0:T(8,128)(2,1)} %bitcast.33, ...), custom_call_target="tpu_custom_call" | custom-call | tf_op jit(solution)/shard_map/gather_raw/pallas_call | solution.py:232
  39.0 14.1 %enter.1 = (bf16[2,512,768]{2,1,0:T(8,128)(2,1)}, bf16[2,768,512]{2,1,0:T(8,128)(2,1)}, bf16[2,528,1792]{2,1,0:T(8,128)(2,1)}, bf16[2,512,1792]{2,1,0:T(8,128)(2...) custom-call(bf16[2,512,768]{2,1,0:T(8,128)(2,1)} %bitcast.34, ...), custom_call_target="tpu_custom_call" | custom-call | tf_op jit(solution)/shard_map/enter/pallas_call | solution.py:359
  53.1 2.3 %collective-permute-start = (bf16[2,1536,128]{2,1,0:T(8,128)(2,1)}, bf16[2,1536,128]{2,1,0:T(8,128)(2,1)S(1)}, u32[]{:S(2)}, u32[]{:S(2)}) collective-permute-start(bf16[2,1536,128]{2,1,0:T(8,128)(2,1)} %get-tuple-element.77.final_ref), channel_id=1, source_target_pairs={{0,1},{2,3},{4,5},{6,7},{8,9},{10,11},{12,13},{14,15},{16,17},{18,... | collective-permute-start | bytes 2359304 | tf_op jit(solution)/shard_map/ppermute | solution.py:1461
  55.5 2.2 collective-permute-done.in_ref
  57.6 0.9 copy-done.1
  58.5 12.2 %forward_scan.1 = (f32[2,1536,512]{2,1,0:T(8,128)}, bf16[2,4,1536,128]{3,2,1,0:T(8,128)(2,1)}) custom-call(bf16[2,1536,512]{2,1,0:T(8,128)(2,1)} %get-tuple-element.74.val_ref.refs_6_, bf16[2,512,256]{2,1,0:T(8,128)(2,1)} %get-tuple-element.75.w_ref.r_ref.refs_7_, bf16[2,512,256]{2,1,0:T(8,128)(2,1)} %get-tuple-element.75.w_ref.r_ref.refs_7_, ...), custom_call_target="tpu_custom_call" | custom-call | tf_op jit(solution)/shard_map/forward_scan/pallas_call | solution.py:432
  70.7 36.5 %leave.1 = (bf16[2,512,768]{2,1,0:T(8,128)(2,1)}, bf16[2,1536,512]{2,1,0:T(8,128)(2,1)}, bf16[2,768,512]{2,1,0:T(8,128)(2,1)}, f32[2,32,512]{2,1,0:T(8,128)}, bf...) custom-call(bf16[8,4,96,768]{3,2,1,0:T(8,128)(2,1)} %bitcast.45, ...), custom_call_target="tpu_custom_call" | custom-call | tf_op jit(solution)/shard_map/leave/pallas_call | solution.py:808
  107.3 1.1 copy-done.5
  108.4 1.3 collective-permute-start.1
  109.7 2.9 %collective-permute-done.1.in_ref = bf16[2,1536,128]{2,1,0:T(8,128)(2,1)S(1)} collective-permute-done((bf16[2,1536,128]{2,1,0:T(8,128)(2,1)S(1)}, bf16[2,1536,128]{2,1,0:T(8,128)(2,1)S(1)}, u32[]{:S(2)}, u32[]{:S(2)}) %collective-permute-start.1) | collective-permute-done | bytes 786464 | tf_op jit(solution)/shard_map/ppermute | solution.py:1465
  112.5 0.9 copy-done
  113.4 21.1 %backward_scan.1 = (bf16[2,1536,512]{2,1,0:T(8,128)(2,1)}, f32[2,512,256]{2,1,0:T(8,128)}, f32[2,32,512]{2,1,0:T(8,128)}, f32[8,128]{1,0:T(8,128)}, f32[2,8,1792]{2,1,0:T(8,128)}) custom-call(bf16[2,1536,512]{2,1,0:T(8,128)(2,1)} %get-tuple-element.74.val_ref.refs_6_, bf16[2,512,256]{2,1,0:T(8,128)(2,1)} %get-tuple-element.75.w_ref.r_ref.refs_7_, ...), custom_call_target="tpu_custom_call" | custom-call | tf_op jit(solution)/shard_map/backward_scan/pallas_call | solution.py:560
  134.5 1.3 collective-permute-start.2
  135.8 2.1 collective-permute-done.2.back_ref
  137.9 0.6 copy-done.4
  138.6 21.5 %leave_back.1 = (bf16[2,512,768]{2,1,0:T(8,128)(2,1)}, bf16[768,1792]{1,0:T(8,128)(2,1)}, f32[32,768]{1,0:T(8,128)}, f32[8,768]{1,0:T(8,128)}, f32[8,1792]{1,0:T(8,128)}) custom-call(bf16[2,1536,512]{2,1,0:T(8,128)(2,1)} %get-tuple-element.87.gval_ref, f32[2,512,256]{2,1,0:T(8,128)} %get-tuple-element.88.gwr_ref, ...), custom_call_target="tpu_custom_call" | custom-call | tf_op jit(solution)/shard_map/leave_back/pallas_call | solution.py:982
  160.0 41.3 %compress.1 = (f32[64,8,128]{2,1,0:T(8,128)}, f32[96,8]{1,0:T(8,128)}, f32[192,8]{1,0:T(8,128)}, f32[8,96]{1,0:T(8,128)}, f32[8,192]{1,0:T(8,128)}, /*index=5*/f32[96,1792]{1,0:T(8,128)}) custom-call(f32[8,3328]{1,0:T(8,128)} %bitcast.51, f32[8,768]{1,0:T(8,128)} %bitcast.52, bf16[8,384,768]{2,1,0:T(8,128)(2,1)} %get-tuple-element.94.grads_ref, ...), custom_call_target="tpu_custom_call" | custom-call | tf_op jit(solution)/shard_map/compress/pallas_call | solution.py:1344
  201.3 0.9 slice.36
  202.2 0.8 slice_bitcast_fusion
  203.0 0.1 reshape.89
  203.1 0.7 copy.30
  203.8 0.8 reshape.87
  204.6 0.7 multiply_subtract_fusion
  205.3 7.5 %finish.1 = (f32[96,3328]{1,0:T(8,128)}, f32[96,3328]{1,0:T(8,128)}, f32[96,3328]{1,0:T(8,128)}, f32[192,768]{1,0:T(8,128)}, f32[192,768]{1,0:T(8,128)}, /*index...) custom-call(f32[64,8,128]{2,1,0:T(8,128)} %get-tuple-element.102.rights_ref, ...), custom_call_target="tpu_custom_call" | custom-call | tf_op jit(solution)/shard_map/finish/pallas_call | solution.py:1437
  (18 shorter events, 0.2 us)
Async XLA Ops:
  7.2 63.6 %all-gather.2.cloned.1.call-start = ((), (), s32[]{:S(2)}) async-start(), calls=%async_computation.1 | async-start | bytes 5308416 | tf_op jit(solution)/shard_map/all_gather | solution.py:1469
  9.7 1.0 copy-start.2
  10.6 194.7 %reduce-scatter.2.cloned.1.call-start = ((), (), s32[]{:S(2)}) async-start(), calls=%async_computation.2 | async-start | bytes 5308416 | tf_op jit(solution)/shard_map/reduce_scatter | solution.py:1473
  53.1 4.5 %collective-permute-start = (bf16[2,1536,128]{2,1,0:T(8,128)(2,1)}, bf16[2,1536,128]{2,1,0:T(8,128)(2,1)S(1)}, u32[]{:S(2)}, u32[]{:S(2)}) collective-permute-start(bf16[2,1536,128]{2,1,0:T(8,128)(2,1)} %get-tuple-element.77.final_ref), channel_id=1, source_target_pairs={{0,1},{2,3},{4,5},{6,7},{8,9},{10,11},{12,13},{14,15},{16,17},{18,... | collective-permute-start | bytes 2359304 | tf_op jit(solution)/shard_map/ppermute | solution.py:1461
  57.6 0.9 copy-start.1
  107.2 1.1 copy-start.5
  108.4 4.2 %collective-permute-start.1 = (bf16[2,1536,128]{2,1,0:T(8,128)(2,1)S(1)}, bf16[2,1536,128]{2,1,0:T(8,128)(2,1)S(1)}, u32[]{:S(2)}, u32[]{:S(2)}) collective-permute-start(bf16[2,1536,128]{2,1,0:T(8,128)(2,1)S(1)} %copy-done.5), channel_id=1, source_target_pairs={{1,0},{3,2},{5,4},{7,6},{9,8},{11,10},{13,12},{15,14},{17,16},{19,... | collective-permute-start | bytes 2359304 | tf_op jit(solution)/shard_map/ppermute | solution.py:1465
  112.5 0.9 copy-start
  134.5 3.4 %collective-permute-start.2 = (f32[2,8,1792]{2,1,0:T(8,128)}, f32[2,8,1792]{2,1,0:T(8,128)S(1)}, u32[]{:S(2)}, u32[]{:S(2)}) collective-permute-start(f32[2,8,1792]{2,1,0:T(8,128)} %get-tuple-element.90), channel_id=1, source_target_pairs={{1,0},{3,2},{5,4},{7,6},{9,8},{11,10},{13,12},{15,14},{17,16},{19,... | collective-permute-start | bytes 344072 | tf_op jit(solution)/shard_map/ppermute | solution.py:1465
  137.9 0.6 copy-start.4
  203.1 1.5 copy-start.3
Sparse Core Ops, SparseCore 0:
  10.7 47.4 all-gather.1
  107.4 54.0 reduce-scatter.1
where the time goes:
time: 220 us
  Pallas kernels  181 us (82%)
  between operations  14.2 us (6%)
  local copies, waits for them, and re-layouts  8.44 us (4%)
  waiting for transfers between devices  7.22 us (3%)
  starting transfers between devices  4.99 us (2%)
  other arithmetic  4.06 us (2%)
    pallas_call x1, Pallas kernels, compress(): pl.pallas_call(partial(compress_kernel, group, replicas), out_shape=[jax....  41.3 us
    pallas_call x1, Pallas kernels, leave(): pl.pallas_call(partial(leave_kernel, group, packed), grid=(n, length // R...  36.5 us
    pallas_call x1, Pallas kernels, gather_raw(): pl.pallas_call(partial(gather_kernel, nf), out_shape=[jax.ShapeDtypeStruc...  26.7 us
    pallas_call x1, Pallas kernels, leave_back(): pl.pallas_call(exit_kernel, grid=(n,), in_specs=[piece(INNER, length), pi...  21.5 us
    pallas_call x1, Pallas kernels, backward_scan(): pl.pallas_call(backward_kernel, grid=(n, chunks), in_specs=[lanes(INNER),...  21.1 us
    pallas_call x1, Pallas kernels, enter(): pl.pallas_call(enter_kernel, grid=(n,), in_specs=[piece(length, D), piece...  14.1 us
    pallas_call x1, Pallas kernels, forward_scan(): pl.pallas_call(forward_kernel, grid=(n,), in_specs=[piece(INNER, length),...  12.2 us
    pallas_call x1, Pallas kernels, finish(): pl.pallas_call(partial(finish_kernel, rates, replicas), grid=(steps,), in...  7.51 us
  transfers between devices with their start and end apart: 5, of which 3 were waited for; matrix products, arithmetic and copies ran while one was open for 3% of the time, Pallas kernels for 62%

commit v1 on v0

--- a/solution.py
+++ b/solution.py
@@ -257,6 +257,32 @@
     return full.reshape(2 * nf * rows, XBC), *rest
 
 
+def store_shift(shift, i, j, values):
+    shift[i, (j - 1) * 128 : j * 128, :] = values
+
+
+def shift_matrices(docs, store):
+    own = docs[0:1, LEAD:]
+    rows = lax.broadcasted_iota(jnp.int32, (128, SPAN), 0)
+    cols = lax.broadcasted_iota(jnp.int32, (128, SPAN), 1)
+    for j in range(1, CONV):
+        same = jnp.where(docs[BEFORE + j : BEFORE + j + 1, LEAD:] == own, 1.0, 0.0)
+        for i in range(own.shape[1] // 128):
+            here = square_of(same[:, i * 128 : i * 128 + 128])
+            here = jnp.concatenate([here, here[:, : SPAN - 128]], axis=1)
+            store(i, j, jnp.where(cols == rows + (HALO - j), here, 0.0).astype(BF16))
+
+
+def step_terms(normed, dlow, heads_ref, docs):
+    length = normed.shape[0]
+    own = docs[0:1, LEAD:]
+    draw = nt(dlow, normed) + column(heads_ref, BIAS)
+    delta = softplus(draw)
+    totals = nn_high(-jnp.exp(column(heads_ref, RATE)) * delta, triangle(length))
+    keep = jnp.where(own == own[:, length - 1 :], 1.0, 0.0)
+    return draw, delta, jnp.exp(totals[:, length - 1 :] - totals) * keep * delta
+
+
 def enter_kernel(
     tok_ref, halo_ref, gain_ref, wraw_ref, dlow_ref, conv_ref, heads_ref, docs_ref,
     normed_ref, turned_ref, raw_ref, dsilu_ref, val_ref, wr_ref, draw_ref, delta_ref, send_ref,
@@ -273,25 +299,10 @@
     normed = ext[HALO:, :]
     normed_ref[0] = normed
     turned_ref[0] = normed.T
-    own = docs_ref[0, 0:1, LEAD:]
-    rows = lax.broadcasted_iota(jnp.int32, (128, SPAN), 0)
-    cols = lax.broadcasted_iota(jnp.int32, (128, SPAN), 1)
-    for j in range(1, CONV):
-        same = jnp.where(docs_ref[0, BEFORE + j : BEFORE + j + 1, LEAD:] == own, 1.0, 0.0)
-        for b in range(0, length, 128):
-            here = square_of(same[:, b : b + 128])
-            here = jnp.concatenate([here, here[:, : SPAN - 128]], axis=1)
-            shift[b // 128, (j - 1) * 128 : j * 128, :] = jnp.where(
-                cols == rows + (HALO - j), here, 0.0
-            ).astype(BF16)
-
-    draw = nt(dlow_ref[...], normed) + column(heads_ref, BIAS)
-    delta = softplus(draw)
+    shift_matrices(docs_ref[0], lambda i, j, values: store_shift(shift, i, j, values))
+    draw, delta, weight = step_terms(normed, dlow_ref[...], heads_ref, docs_ref[0])
     draw_ref[0] = draw
     delta_ref[0] = delta
-    totals = nn_high(-jnp.exp(column(heads_ref, RATE)) * delta, triangle(length))
-    keep = jnp.where(own == own[:, length - 1 :], 1.0, 0.0)
-    weight = jnp.exp(totals[:, length - 1 :] - totals) * keep * delta
     tiles = XBC // TILE
     blocks = length // 128
 
@@ -300,13 +311,13 @@
 
     def project(c):
         if c < tiles:
-            raw_ref[0, :, span_of(c)] = nn(ext[...], wraw_ref[:, span_of(c)]).astype(BF16)
+            raw_ref[0, c] = nn(ext[...], wraw_ref[c]).astype(BF16)
 
     def move(c):
         if c < tiles:
             for i in range(blocks):
                 moved[c % 2 * blocks + i] = nn(
-                    shift[i], raw_ref[0, i * 128 : i * 128 + SPAN, span_of(c)]
+                    shift[i], raw_ref[0, c, i * 128 : i * 128 + SPAN, :]
                 )
 
     project(0)
@@ -323,14 +334,14 @@
                 lanes = slice(half, half + 128)
                 w = conv_ref[:, hc]
                 for q in range(0, 128, 64):
-                    z = w[4:5] + w[3:4] * raw_ref[0, HALO + b + q : HALO + b + q + 64, hc].astype(F32)
+                    z = w[4:5] + w[3:4] * raw_ref[0, c, HALO + b + q : HALO + b + q + 64, lanes].astype(F32)
                     for j in range(1, CONV):
                         at = (j - 1) * 128 + q
                         z = z + w[3 - j : 4 - j] * moved[slot, at : at + 64, lanes]
                     sig = sigmoid(z)
                     silu = z * sig
                     act[c % 2, b + q : b + q + 64, lanes] = silu
-                    dsilu_ref[0, b + q : b + q + 64, hc] = (sig + silu * (1.0 - sig)).astype(BF16)
+                    dsilu_ref[0, c, b + q : b + q + 64, lanes] = (sig + silu * (1.0 - sig)).astype(BF16)
         if c < INNER // TILE:
             val_ref[0, span, :] = act[c % 2].T.astype(BF16)
         else:
@@ -348,8 +359,8 @@
     outs = [
         ((n, length, D), BF16),
         ((n, D, length), BF16),
-        ((n, length + HALO, XBC), BF16),
-        ((n, length, XBC), BF16),
+        ((n, XBC // TILE, length + HALO, TILE), BF16),
+        ((n, XBC // TILE, length, TILE), BF16),
         ((n, INNER, length), BF16),
         ((n, length, 2 * STATE), BF16),
         ((n, HP, length), F32),
@@ -374,6 +385,218 @@
         compiler_params=params(("arbitrary",)),
         name="enter",
     )(tokens, halo, gain, wraw, dlow, conv, heads, docs)
+
+
+class Copies:
+    def __init__(self, *semaphores):
+        self.semaphores, self.copies = semaphores, []
+
+    def local(self, src, dst):
+        copy = pltpu.make_async_copy(src, dst, self.semaphores[0].at[len(self.copies)])
+        copy.start()
+        self.copies.append(copy)
+        return copy
+
+    def remote(self, src, dst, device):
+        k = len(self.copies)
+        copy = pltpu.make_async_remote_copy(
+            src, dst, self.semaphores[0].at[k], self.semaphores[1].at[k],
+            device_id=device, device_id_type=MESH,
+        )
+        copy.start()
+        self.copies.append(copy)
+        return copy
+
+
+def front_kernel(
+    w_ref, tok_ref, small_ref, seg_ref, dlow_ref,
+    wraw_ref, normed_ref, turned_ref, raw_ref, dsilu_ref, val_ref, wr_ref, draw_ref, delta_ref,
+    send_ref, come_ref, conv_ref, gate_ref, heads_ref, docs_ref,
+    mine, near, halo, wide, gain, ext, turned, raw, dsilu, val, moved, act, shift, weight,
+    stored, send, recv,
+):
+    r, f, s = lax.axis_index("rep"), lax.axis_index("fsdp"), lax.axis_index("seq")
+    fx, fy = f + 1 - 2 * lax.rem(f, 2), lax.rem(f + 2, 4)
+    fd = lax.rem(fx + 2, 4)
+    x_dev, y_dev, other = (r, fx, s), (r, fy, s), (r, f, 1 - s)
+    pieces, length, _ = tok_ref.shape
+    tiles, blocks = XBC // TILE, length // 128
+    order = [tiles - 1, *range(tiles - 1)]
+    barrier = pltpu.get_barrier_semaphore()
+    for device in (x_dev, y_dev, other):
+        pl.semaphore_signal(barrier, inc=1, device_id=device, device_id_type=MESH)
+    for c in range(tiles):
+        mine[c] = w_ref[:, INNER + c * TILE : INNER + (c + 1) * TILE].astype(BF16)
+    near[...] = tok_ref[:, length - HALO :, :]
+    pl.semaphore_wait(barrier, 3)
+    outward, out = Copies(send, recv), Copies(stored)
+    arriving = {}
+
+    def block(c, owner):
+        return wide.at[c, owner * 2 + s]
+
+    def offer(at):
+        if at < tiles:
+            c = order[at]
+            arriving[c] = [
+                outward.remote(mine.at[c], block(c, f), device) for device in (x_dev, y_dev, other)
+            ]
+            wide[c, f * 2 + s] = mine[c]
+
+    def relay(at):
+        if at < tiles:
+            c = order[at]
+            from_x, from_y, _ = arriving[c]
+            from_x.wait_recv()
+            from_y.wait_recv()
+            through = (fx, y_dev) if at % 2 == 0 else (fy, x_dev)
+            across = block(c, through[0])
+            arriving[c].append(outward.remote(across, across, through[1]))
+            for owner in (fx, fy):
+                arriving[c].append(outward.remote(block(c, owner), block(c, owner), other))
+
+    def finish_tile(at):
+        c = order[at]
+        arriving[c][3].wait_recv()
+        arriving[c].append(outward.remote(block(c, fd), block(c, fd), other))
+        for k in (2, 4, 5, 6):
+            arriving[c][k].wait_recv()
+        out.local(wide.at[c], wraw_ref.at[c])
+
+    bring_halo = outward.remote(near, halo, other)
+    offer(0)
+    offer(1)
+    offer(2)
+    unpack_small(small_ref, gain, conv_ref, gate_ref, heads_ref)
+    unpack_documents(seg_ref, docs_ref, s == 1)
+    bring_halo.wait_recv()
+    for n in range(pieces):
+        x = halo[n].astype(F32)
+        scale = lax.rsqrt(jnp.mean(x * x, axis=-1, keepdims=True) + EPS)
+        ext[n, :HALO, :] = (x * scale * gain[...]).astype(BF16)
+    for n in range(pieces):
+        if n == pieces - 1:
+            relay(0)
+        for b in range(0, length, 128):
+            x = tok_ref[n, b : b + 128, :].astype(F32)
+            scale = lax.rsqrt(jnp.mean(x * x, axis=-1, keepdims=True) + EPS)
+            ext[n, HALO + b : HALO + b + 128, :] = (x * scale * gain[...]).astype(BF16)
+        out.local(ext.at[n, pl.ds(HALO, length)], normed_ref.at[n])
+        turned[n] = ext[n, HALO:, :].T
+        out.local(turned.at[n], turned_ref.at[n])
+        draw_ref[n], delta_ref[n], weight[n] = step_terms(
+            ext[n, HALO:, :], dlow_ref[...], heads_ref, docs_ref[n]
+        )
+        shift_matrices(
+            docs_ref[n], lambda i, j, values: store_shift(shift, n * blocks + i, j, values)
+        )
+    states = []
+    for at, c in enumerate(order):
+        relay(at + 1)
+        offer(at + 3)
+        finish_tile(at)
+        columns = wide[c].reshape(D, TILE)
+        for n in range(pieces):
+            raw[n, c] = nn(ext[n], columns).astype(BF16)
+            out.local(raw.at[n, c], raw_ref.at[n, c])
+        for n in range(pieces):
+            for i in range(blocks):
+                moved[n * blocks + i] = nn(
+                    shift[n * blocks + i], raw[n, c, i * 128 : i * 128 + SPAN, :]
+                )
+        for n in range(pieces):
+            for b in range(0, length, 128):
+                slot = n * blocks + b // 128
+                for half in range(0, TILE, 128):
+                    hc = slice(c * TILE + half, c * TILE + half + 128)
+                    lanes = slice(half, half + 128)
+                    w = conv_ref[:, hc]
+                    for q in range(0, 128, 64):
+                        here = raw[n, c, HALO + b + q : HALO + b + q + 64, lanes].astype(F32)
+                        z = w[4:5] + w[3:4] * here
+                        for j in range(1, CONV):
+                            row = (j - 1) * 128 + q
+                            z = z + w[3 - j : 4 - j] * moved[slot, row : row + 64, lanes]
+                        sig = sigmoid(z)
+                        silu = z * sig
+                        act[n, b + q : b + q + 64, lanes] = silu
+                        dsilu[n, c, b + q : b + q + 64, lanes] = (
+                            sig + silu * (1.0 - sig)
+                        ).astype(BF16)
+            out.local(dsilu.at[n, c], dsilu_ref.at[n, c])
+            if c == tiles - 1:
+                wr_ref[n] = act[n].astype(BF16)
+                continue
+            rows = slice(c * TILE, (c + 1) * TILE)
+            val[n, rows, :] = act[n].T.astype(BF16)
+            out.local(val.at[n, rows], val_ref.at[n, rows])
+            writers = wr_ref[n, :, :STATE]
+            for h in range(c * 4, c * 4 + 4):
+                head = slice(h * HEADDIM, (h + 1) * HEADDIM)
+                scaled = val[n, head, :].astype(F32) * weight[n, h : h + 1, :]
+                send_ref[n, head, :] = nn(scaled.astype(BF16), writers).astype(BF16)
+            states.append(outward.remote(send_ref.at[n, rows], come_ref.at[n, rows], other))
+    for copy in states:
+        copy.wait_recv()
+    for copy in outward.copies:
+        copy.wait_send()
+    for copy in out.copies:
+        copy.wait()
+
+
+def front(weight, tokens, small_rows, segments, dlow):
+    rows = weight.shape[0]
+    n, length, _ = tokens.shape
+    tiles, blocks = XBC // TILE, length // 128
+    vmem, hbm = pl.BlockSpec(memory_space=pltpu.VMEM), pl.BlockSpec(memory_space=pl.ANY)
+    outs = [
+        (hbm, (tiles, 8, rows, TILE), BF16),
+        (hbm, (n, length, D), BF16),
+        (hbm, (n, D, length), BF16),
+        (hbm, (n, tiles, length + HALO, TILE), BF16),
+        (hbm, (n, tiles, length, TILE), BF16),
+        (hbm, (n, INNER, length), BF16),
+        (vmem, (n, length, 2 * STATE), BF16),
+        (vmem, (n, HP, length), F32),
+        (vmem, (n, HP, length), F32),
+        (vmem, (n, INNER, STATE), BF16),
+        (vmem, (n, INNER, STATE), BF16),
+        (vmem, (CONV + 1, XBC), F32),
+        (vmem, (INNER // 128, 128), F32),
+        (vmem, (8, 128), F32),
+        (vmem, (n, 8, LEAD + length), F32),
+    ]
+    remote = 1 + 7 * tiles + n * (tiles - 1)
+    local = tiles + 2 * n + 2 * n * tiles + n * (tiles - 1)
+    return pl.pallas_call(
+        front_kernel,
+        in_specs=[vmem] * 5,
+        out_specs=[spec for spec, _, _ in outs],
+        out_shape=[jax.ShapeDtypeStruct(shape, kind) for _, shape, kind in outs],
+        scratch_shapes=[
+            pltpu.VMEM((tiles, rows, TILE), BF16),
+            pltpu.VMEM((n, HALO, D), BF16),
+            pltpu.VMEM((n, HALO, D), BF16),
+            pltpu.VMEM((tiles, 8, rows, TILE), BF16),
+            pltpu.VMEM((1, D), F32),
+            pltpu.VMEM((n, length + HALO, D), BF16),
+            pltpu.VMEM((n, D, length), BF16),
+            pltpu.VMEM((n, tiles, length + HALO, TILE), BF16),
+            pltpu.VMEM((n, tiles, length, TILE), BF16),
+            pltpu.VMEM((n, INNER, length), BF16),
+            pltpu.VMEM((n * blocks, (CONV - 1) * 128, TILE), F32),
+            pltpu.VMEM((n, length, TILE), F32),
+            pltpu.VMEM((n * blocks, (CONV - 1) * 128, SPAN), BF16),
+            pltpu.VMEM((n, HP, length), F32),
+            pltpu.SemaphoreType.DMA((local,)),
+            pltpu.SemaphoreType.DMA((remote,)),
+            pltpu.SemaphoreType.DMA((remote,)),
+        ],
+        compiler_params=pltpu.CompilerParams(
+            collective_id=3, has_side_effects=True, vmem_limit_bytes=VMEM_LIMIT
+        ),
+        name="front",
+    )(weight, tokens, small_rows, segments, dlow)
 
 
 def chunk_terms(delta, rate, docs):
@@ -399,7 +622,7 @@
     y_ref, start_ref,
     state, off, fresh,
 ):
-    state[...] = in_ref[0].astype(F32)
+    state[...] = jnp.where(lax.axis_index("seq") == 0, 0.0, in_ref[0].astype(F32))
     rate = column(heads_ref, RATE)
     for k in range(val_ref.shape[2] // CH):
         lanes = slice(k * CH, (k + 1) * CH)
@@ -535,7 +758,8 @@
                 here = gval_ref[0, cols, :].astype(F32).T[:8, :]
             else:
                 here = gwr_ref[0, 0:8, c * 128 - INNER : c * 128 - INNER + 128]
-            pre = here * dsilu_ref[0, 0:8, cols].astype(F32)
+            left = c * 128 % TILE
+            pre = here * dsilu_ref[0, c * 128 // TILE, 0:8, left : left + 128].astype(F32)
             wide = jnp.concatenate([jnp.zeros((8, 128), F32), pre], axis=0)
             total = jnp.zeros((8, 128), F32)
             for j in range(1, CONV):
@@ -573,7 +797,7 @@
             pl.BlockSpec((1, 1, INNER, STATE), lambda i, k: (i, back(k), 0, 0)),
             pl.BlockSpec((1, INNER, STATE), lambda i, k: (i, 0, 0)),
             pl.BlockSpec((1, INNER, STATE), lambda i, k: (i, 0, 0)),
-            pl.BlockSpec((1, 16, XBC), lambda i, k: (i, 0, 0)),
+            pl.BlockSpec((1, XBC // TILE, 16, TILE), lambda i, k: (i, 0, 0, 0)),
             whole(conv.shape, 2),
             pl.BlockSpec((1, 8, 128), lambda i, k: (i, 0, 0)),
         ],
@@ -855,7 +1079,7 @@
     pre, low_pre, moved, halo_terms, shift, low, lifted, total, sums,
 ):
     n = pl.program_id(0)
-    length = dsilu_ref.shape[1]
+    length = dsilu_ref.shape[2]
     last = n == pl.num_programs(0) - 1
 
     @pl.when(n == 0)
@@ -898,7 +1122,7 @@
             here = gval_ref[0, span_of(c), :].astype(F32).T
         else:
             here = gwr_ref[0]
-        here = here * dsilu_ref[0, :, span_of(c)].astype(F32)
+        here = here * dsilu_ref[0, c].astype(F32)
         pre[c % 2] = here
         low_pre[c % 2, HALO : HALO + length, :] = here.astype(BF16)
         halo_terms[c % 2] = nn(ahead, low_pre[c % 2, : 2 * HALO, :])
@@ -909,7 +1133,7 @@
 
     def close_tile(c):
         total[:, span_of(c)] += nn(turned_ref[0], low[c % 2])
-        through = nt(low[c % 2], wraw_ref[:, span_of(c)])
+        through = nt(low[c % 2], wraw_ref[c])
         if c == 0:
             lifted[...] = through
         else:
@@ -929,12 +1153,12 @@
             wide = slice(c * TILE + half, c * TILE + half + 128)
             w = conv_ref[:, wide]
             folded = [sums[k, :, wide] for k in range(CONV + 1)]
-            raw = raw_ref[0, :HALO, wide].astype(F32)
+            raw = raw_ref[0, c, :HALO, cols].astype(F32)
             for j in range(1, CONV):
                 term = halo_terms[slot, (j - 1) * HALO : j * HALO, cols]
                 folded[3 - j] = folded[3 - j] + fold(raw * term)
             for b in range(0, length, 64):
-                raw = raw_ref[0, HALO + b : HALO + b + 64, wide].astype(F32)
+                raw = raw_ref[0, c, HALO + b : HALO + b + 64, cols].astype(F32)
                 now = pre[slot, b : b + 64, cols]
                 grad = w[3:4] * now
                 folded[3] = folded[3] + fold(raw * now)
@@ -978,13 +1202,13 @@
     gval, gwr, dsilu, raw, docs, conv, back, normed, turned, wraw, gdraw, dlow, gnorm, tokens,
     cotangent, gain,
 ):
-    n, length, _ = dsilu.shape
+    n, length, _ = tokens.shape
     return pl.pallas_call(
         exit_kernel,
         grid=(n,),
         in_specs=[
-            piece(INNER, length), piece(length, 2 * STATE), piece(length, XBC),
-            piece(length + HALO, XBC), piece(*docs.shape[1:]), whole(conv.shape), piece(8, XBC),
+            piece(INNER, length), piece(length, 2 * STATE), piece(XBC // TILE, length, TILE),
+            piece(XBC // TILE, length + HALO, TILE), piece(*docs.shape[1:]), whole(conv.shape), piece(8, XBC),
             piece(length, D), piece(D, length), whole(wraw.shape), piece(HP, length),
             whole(dlow.shape), piece(D, length), piece(length, D), piece(length, D),
             whole(gain.shape),
@@ -1505,13 +1729,24 @@
     weights = gather_rows(weights).reshape(group, 4, -1, D)
     delta_rows = small_values[D:AT_CONV].reshape(D, HEADS).astype(BF16).T
     delta_rows = jnp.pad(delta_rows, ((0, HP - HEADS), (0, 0)))
-    raw_full, halo, norm_gain, conv, gate_gain, heads, docs = gather_raw(
-        input_weight, tokens, small_rows, segments.reshape(pieces, 1, segments.shape[2])
-    )
-    normed, turned, raw, dsilu, values, wr, draw, delta, send = enter(
-        tokens, halo, norm_gain, raw_full, delta_rows, conv, heads, docs
-    )
-    y, starts = forward_scan(values, wr, delta, heads, docs, to_later(send))
+    segments = segments.reshape(pieces, 1, segments.shape[2])
+    norm_gain = small_values[:D].reshape(1, D)
+    if lax.axis_size("fsdp") == 4 and input_weight.shape[0] % 16 == 0:
+        (
+            raw_full, normed, turned, raw, dsilu, values, wr, draw, delta, send, come,
+            conv, gate_gain, heads, docs,
+        ) = front(input_weight, tokens, small_rows, segments, delta_rows)
+        raw_full = raw_full.reshape(XBC // TILE, D, TILE)
+    else:
+        raw_full, halo, _, conv, gate_gain, heads, docs = gather_raw(
+            input_weight, tokens, small_rows, segments
+        )
+        raw_full = raw_full.reshape(D, XBC // TILE, TILE).transpose(1, 0, 2)
+        normed, turned, raw, dsilu, values, wr, draw, delta, send = enter(
+            tokens, halo, norm_gain, raw_full, delta_rows, conv, heads, docs
+        )
+        come = to_later(send)
+    y, starts = forward_scan(values, wr, delta, heads, docs, come)
     output, gy, gnorm, first, gstate, grads, ggate, gskip = leave(
         weights, normed, turned, cotangent, tokens, y, values, wr, gate_gain, delta, heads, docs
     )

time: 220 us -> 226 us (1.027); the launches traced: 220 us -> 223 us
  Pallas kernels: 181 us -> 190 us
  waiting for transfers between devices: 7.22 us -> 4.46 us
  starting transfers between devices: 4.99 us -> 2.65 us
    pallas_call x2 -> x1, Pallas kernels: 40.7 us -> 48.7 us  [front(): pl.pallas_call(front_kernel, in_specs=[vmem] * 5, out_specs=[spec for spe...]
    ppermute x1 -> x0, starting transfers between devices: 2.34 us -> none  [to_later(): lax.ppermute(block, 'seq', [(i, i + 1) for i in range(lax.axis_size('seq'...]
  transfers between devices with their start and end apart: 5 -> 4, of which waited for: 3 -> 2; matrix products, arithmetic and copies ran while one was open for 3% -> 3% of each run, Pallas kernels for 62% -> 65%
where the time goes in v1:
time: 226 us; the launch traced here: 223 us
  Pallas kernels  190 us (84%)
  between operations  14.7 us (7%)
  local copies, waits for them, and re-layouts  8.16 us (4%)
  waiting for transfers between devices  4.46 us (2%)
  other arithmetic  3.04 us (1%)
  starting transfers between devices  2.65 us (1%)
    pallas_call x1, Pallas kernels, front(): pl.pallas_call(front_kernel, in_specs=[vmem] * 5, out_specs=[spec for spe...  48.7 us
    pallas_call x1, Pallas kernels, compress(): pl.pallas_call(partial(compress_kernel, group, replicas), out_shape=[jax....  42.1 us
    pallas_call x1, Pallas kernels, leave(): pl.pallas_call(partial(leave_kernel, group, packed), grid=(n, length // R...  36.4 us
    pallas_call x1, Pallas kernels, leave_back(): pl.pallas_call(exit_kernel, grid=(n,), in_specs=[piece(INNER, length), pi...  21.6 us
    pallas_call x1, Pallas kernels, backward_scan(): pl.pallas_call(backward_kernel, grid=(n, chunks), in_specs=[lanes(INNER),...  21.1 us
    pallas_call x1, Pallas kernels, forward_scan(): pl.pallas_call(forward_kernel, grid=(n,), in_specs=[piece(INNER, length),...  12.2 us
    pallas_call x1, Pallas kernels, finish(): pl.pallas_call(partial(finish_kernel, rates, replicas), grid=(steps,), in...  7.51 us
  transfers between devices with their start and end apart: 4, of which 2 were waited for; matrix products, arithmetic and copies ran while one was open for 3% of the time, Pallas kernels for 65%

profile of v1, /device:TPU:0, one launch (start us, length us, event | category | flops | bytes accessed | tf_op | source)
XLA Modules:
  0.0 222.7 jit_solution(9025519171078798022)
XLA Ops:
  7.2 0.0 all-gather.2.cloned.1.call-start
  7.2 1.4 convert.13
  8.8 0.9 pad_maximum_fusion
  9.6 0.0 all-gather.2.cloned.1.call-update
  9.6 0.0 reduce-scatter.2.cloned.1.call-start
  9.7 0.3 convert_element_type.9
  10.0 0.1 copy.29
  10.1 0.6 pad.9.dlow_ref
  10.7 0.7 pad_bitcast_fusion.small_ref
  11.4 48.7 %front.1 = (bf16[7,8,96,256]{3,2,1,0:T(8,128)(2,1)}, bf16[2,512,768]{2,1,0:T(8,128)(2,1)}, bf16[2,768,512]{2,1,0:T(8,128)(2,1)}, bf16[2,7,528,256]{3,2,1,0:T(8,1...) custom-call(f32[96,3328]{1,0:T(8,128)} %win_ref.1, ...), custom_call_target="tpu_custom_call" | custom-call | tf_op jit(solution)/shard_map/front/pallas_call | solution.py:571
  60.2 12.2 %forward_scan.1 = (f32[2,1536,512]{2,1,0:T(8,128)}, bf16[2,4,1536,128]{3,2,1,0:T(8,128)(2,1)}) custom-call(bf16[2,1536,512]{2,1,0:T(8,128)(2,1)} %get-tuple-element.67.val_ref.refs_6_, bf16[2,512,256]{2,1,0:T(8,128)(2,1)} %get-tuple-element.68.w_ref.r_ref.refs_7_, bf16[2,512,256]{2,1,0:T(8,128)(2,1)} %get-tuple-element.68.w_ref.r_ref.refs_7_, ...), custom_call_target="tpu_custom_call" | custom-call | tf_op jit(solution)/shard_map/forward_scan/pallas_call | solution.py:655
  72.4 0.0 all-gather.2.cloned.1.call-done
  72.4 36.4 %leave.1 = (bf16[2,512,768]{2,1,0:T(8,128)(2,1)}, bf16[2,1536,512]{2,1,0:T(8,128)(2,1)}, bf16[2,768,512]{2,1,0:T(8,128)(2,1)}, f32[2,32,512]{2,1,0:T(8,128)}, bf...) custom-call(bf16[8,4,96,768]{3,2,1,0:T(8,128)(2,1)} %bitcast.42, ...), custom_call_target="tpu_custom_call" | custom-call | tf_op jit(solution)/shard_map/leave/pallas_call | solution.py:1032
  108.8 0.0 reduce-scatter.2.cloned.1.call-update
  108.9 1.1 copy-done.5
  110.0 1.3 collective-permute-start
  111.2 2.9 %collective-permute-done.in_ref = bf16[2,1536,128]{2,1,0:T(8,128)(2,1)S(1)} collective-permute-done((bf16[2,1536,128]{2,1,0:T(8,128)(2,1)S(1)}, bf16[2,1536,128]{2,1,0:T(8,128)(2,1)S(1)}, u32[]{:S(2)}, u32[]{:S(2)}) %collective-permute-start) | collective-permute-done | bytes 786464 | tf_op jit(solution)/shard_map/ppermute | solution.py:1689
  114.1 0.9 copy-done.1
  115.0 21.1 %backward_scan.1 = (bf16[2,1536,512]{2,1,0:T(8,128)(2,1)}, f32[2,512,256]{2,1,0:T(8,128)}, f32[2,32,512]{2,1,0:T(8,128)}, f32[8,128]{1,0:T(8,128)}, f32[2,8,1792]{2,1,0:T(8,128)}) custom-call(bf16[2,1536,512]{2,1,0:T(8,128)(2,1)} %get-tuple-element.67.val_ref.refs_6_, bf16[2,512,256]{2,1,0:T(8,128)(2,1)} %get-tuple-element.68.w_ref.r_ref.refs_7_, ...), custom_call_target="tpu_custom_call" | custom-call | tf_op jit(solution)/shard_map/backward_scan/pallas_call | solution.py:784
  136.1 1.3 collective-permute-start.1
  137.4 0.6 reshape.84.gain_ref
  138.0 1.5 collective-permute-done.1.back_ref
  139.5 0.6 copy-done.4
  140.2 21.6 %leave_back.1 = (bf16[2,512,768]{2,1,0:T(8,128)(2,1)}, bf16[768,1792]{1,0:T(8,128)(2,1)}, f32[32,768]{1,0:T(8,128)}, f32[8,768]{1,0:T(8,128)}, f32[8,1792]{1,0:T(8,128)}) custom-call(bf16[2,1536,512]{2,1,0:T(8,128)(2,1)} %get-tuple-element.84.gval_ref, f32[2,512,256]{2,1,0:T(8,128)} %get-tuple-element.85.gwr_ref, ...), custom_call_target="tpu_custom_call" | custom-call | tf_op jit(solution)/shard_map/leave_back/pallas_call | solution.py:1206
  161.8 42.1 %compress.1 = (f32[64,8,128]{2,1,0:T(8,128)}, f32[96,8]{1,0:T(8,128)}, f32[192,8]{1,0:T(8,128)}, f32[8,96]{1,0:T(8,128)}, f32[8,192]{1,0:T(8,128)}, /*index=5*/f32[96,1792]{1,0:T(8,128)}) custom-call(f32[8,3328]{1,0:T(8,128)} %bitcast.49, f32[8,768]{1,0:T(8,128)} %bitcast.50, bf16[8,384,768]{2,1,0:T(8,128)(2,1)} %get-tuple-element.92.grads_ref, ...), custom_call_target="tpu_custom_call" | custom-call | tf_op jit(solution)/shard_map/compress/pallas_call | solution.py:1568
  203.9 0.9 slice.40
  204.8 0.7 copy.30
  205.5 0.8 reshape.91
  206.3 0.8 slice_bitcast_fusion
  207.1 0.1 reshape.93
  207.2 0.7 multiply_subtract_fusion
  207.9 7.5 %finish.1 = (f32[96,3328]{1,0:T(8,128)}, f32[96,3328]{1,0:T(8,128)}, f32[96,3328]{1,0:T(8,128)}, f32[192,768]{1,0:T(8,128)}, f32[192,768]{1,0:T(8,128)}, /*index...) custom-call(f32[64,8,128]{2,1,0:T(8,128)} %get-tuple-element.100.rights_ref, ...), custom_call_target="tpu_custom_call" | custom-call | tf_op jit(solution)/shard_map/finish/pallas_call | solution.py:1661
  (18 shorter events, 0.1 us)
Async XLA Ops:
  7.2 1.5 copy-start
  7.2 65.2 %all-gather.2.cloned.1.call-start = ((), (), s32[]{:S(2)}) async-start(), calls=%async_computation.1 | async-start | bytes 5308416 | tf_op jit(solution)/shard_map/all_gather | solution.py:1693
  8.7 1.0 copy-start.2
  9.6 198.3 %reduce-scatter.2.cloned.1.call-start = ((), (), s32[]{:S(2)}) async-start(), calls=%async_computation.2 | async-start | bytes 5308416 | tf_op jit(solution)/shard_map/reduce_scatter | solution.py:1697
  108.8 1.1 copy-start.5
  110.0 4.2 %collective-permute-start = (bf16[2,1536,128]{2,1,0:T(8,128)(2,1)S(1)}, bf16[2,1536,128]{2,1,0:T(8,128)(2,1)S(1)}, u32[]{:S(2)}, u32[]{:S(2)}) collective-permute-start(bf16[2,1536,128]{2,1,0:T(8,128)(2,1)S(1)} %copy-done.5), channel_id=1, source_target_pairs={{1,0},{3,2},{5,4},{7,6},{9,8},{11,10},{13,12},{15,14},{17,16},{19,... | collective-permute-start | bytes 2359304 | tf_op jit(solution)/shard_map/ppermute | solution.py:1689
  114.1 0.9 copy-start.1
  115.0 22.4 %slice-start = ((f32[29768]{0:T(1024)}), f32[768]{0:T(1024)S(1)}, s32[]{:S(2)}) async-start(f32[29768]{0:T(1024)} %param.18), calls=%async_computation.3 | async-start | bytes 8192 | tf_op jit(solution)/shard_map/slice | solution.py:1733
  136.1 3.4 %collective-permute-start.1 = (f32[2,8,1792]{2,1,0:T(8,128)}, f32[2,8,1792]{2,1,0:T(8,128)S(1)}, u32[]{:S(2)}, u32[]{:S(2)}) collective-permute-start(f32[2,8,1792]{2,1,0:T(8,128)} %get-tuple-element.87), channel_id=1, source_target_pairs={{1,0},{3,2},{5,4},{7,6},{9,8},{11,10},{13,12},{15,14},{17,16},{19,... | collective-permute-start | bytes 344072 | tf_op jit(solution)/shard_map/ppermute | solution.py:1689
  139.5 0.6 copy-start.4
  204.8 2.3 %copy-start.3 = (f32[29768]{0:T(1024)S(1)}, f32[29768]{0:T(1024)}, u32[]{:S(2)}) copy-start(f32[29768]{0:T(1024)} %param.21) | copy-start | bytes 357220
Sparse Core Ops, SparseCore 0:
  10.5 45.6 all-gather.1
  109.0 54.0 reduce-scatter.1
